TPU v7x, 32 devices: a whole 2x2x4 slice. The times are simulated.
32 devices in a mesh: grp: 2 (over y), sub: 4 (over z), chan: 4 (over x, core).
Axes of the slice: x: 2, y: 2, z: 4, core: 2. Of those that a mesh axis runs over, the one named last changes fastest.
Arguments:
- visibilities: bfloat16 [4, 32, 8, 2, 1024], P('chan', ('grp', 'sub')), parts along dimension 1, may hold values from -6 to 6
- tracks: float32 [32, 2, 128], P(('grp', 'sub')), parts along dimension 0, may hold values from -102 to 102
- freq_ratio: float32 [8, 64], P(('grp', 'chan')), parts along dimension 0, may hold values from 0.9 to 1.1
- blocks_used: int32 [32], P(('grp', 'sub')), parts along dimension 0, may hold values from 2 to 8, as said below
- subgrid_row: int32 [32], P(('grp', 'sub')), parts along dimension 0, may hold values from 0 to 15, as said below
- station_pair: int32 [32, 2], P(('grp', 'sub')), parts along dimension 0, may hold values from 0 to 127
- subgrid_offsets: int32 [32, 2], P(('grp', 'sub')), parts along dimension 0, may hold values from -90 to 90
- aterm_screens: bfloat16 [4, 256, 2, 1024], P('chan', ('grp', 'sub')), parts along dimension 1, may hold values from -4.1875 to 4.1875
Outputs:
- uv_subgrids: float32 [4, 32, 2, 1024], P('chan', ('grp', 'sub')), parts along dimension 1
There are 2 independent parts, one for each index of `grp`. A program takes and returns all parts, laid end to end along the dimension named above; each array names one. Nothing has to cross between parts.
Inputs may be any that keep to these rules, and one draw needn't show every extreme that they name: `blocks_used`: time blocks from this count on hold no data and are left out. `subgrid_row`: A permutation of the 16 rows; row r lies on device r // 4 of sub. The used blocks of one device's baselines whose rows lie on one device number at most 8; the used blocks whose rows lie on one device number at most 26; one device's baselines hold at most 16 used blocks.
All inputs are finite; a program needn't handle non-finite values.
Results may differ from a plain program's by a relative error of at most 0.0047.
Values may be sent and summed in bfloat16 or wider, within the bound.
No kernel may reach another device: no remote copies, remote signals or barrier semaphores. Data moves between devices by JAX's collectives and lax.ppermute only.
A program may use at most 64 MiB of HBM per device.

v0:
```python
import math

import jax
import jax.numpy as jnp
from jax import lax
from jax.sharding import PartitionSpec as P

SUB = 32
BPP = 1


TWO_PI = 2.0 * math.pi


def blocks_to_images(block_vis, block_tracks, centre, ratio_row):
    block_total = block_vis.shape[0]
    sample_count = block_vis.shape[-1]
    steps_time = block_tracks.shape[-1]
    side_len = SUB
    coords = jnp.arange(side_len, dtype=jnp.float32) - side_len // 2
    norm_scale = sample_count ** (-0.5)

    def one_group(group_items):
        group_vis, group_tracks, group_centre = group_items
        group_size = group_vis.shape[0]
        scaled = (
            group_tracks[:, :, None, :] * ratio_row[None, None, :, None]
            - group_centre[:, :, None, None]
        )
        phase_rate = (scaled * (TWO_PI / side_len)).reshape(group_size, 2, sample_count)
        angles = phase_rate[:, :, None, :] * coords[None, None, :, None]
        cosine = jnp.cos(angles)
        sine_table = jnp.sin(angles)
        vis_real = group_vis[:, 0].astype(jnp.float32)[:, None, :]
        vis_imag = group_vis[:, 1].astype(jnp.float32)[:, None, :]
        left_real = (vis_real * cosine[:, 0] - vis_imag * sine_table[:, 0]).astype(jnp.bfloat16)
        left_imag = (vis_real * sine_table[:, 0] + vis_imag * cosine[:, 0]).astype(jnp.bfloat16)
        right_real = cosine[:, 1].astype(jnp.bfloat16)
        right_imag = sine_table[:, 1].astype(jnp.bfloat16)
        left_side = jnp.concatenate([left_real, left_imag], axis=-1)
        right_side = jnp.concatenate(
            [
                jnp.concatenate([right_real, -right_imag], axis=-1),
                jnp.concatenate([right_imag, right_real], axis=-1),
            ],
            axis=1,
        )
        products = jnp.einsum(
            "glk,gnk->gln", left_side, right_side, preferred_element_type=jnp.float32
        )
        image_real = (products[:, :, :side_len] * norm_scale).reshape(
            group_size, side_len * side_len
        )
        image_imag = (products[:, :, side_len:] * norm_scale).reshape(
            group_size, side_len * side_len
        )
        return jnp.stack([image_real, image_imag], axis=1).astype(jnp.bfloat16)

    groups = block_total // 8
    images = lax.map(
        one_group,
        (
            block_vis.reshape(groups, 8, 2, sample_count),
            block_tracks.reshape(groups, 8, 2, steps_time),
            centre.reshape(groups, 8, 2),
        ),
    )
    return images.reshape(block_total, 2, side_len * side_len)


def lookup(table_rows, wanted):
    match = wanted[:, None] == jnp.arange(table_rows.shape[0], dtype=jnp.int32)[None, :]
    return jnp.sum(jnp.where(match[:, :, None], table_rows[None, :, :], 0), axis=1).astype(
        jnp.float32
    )


def packing_result(present_mask, segment_length, marker_index):
    place = jnp.cumsum(present_mask.astype(jnp.int32)) - 1
    target = jnp.where(present_mask, place, segment_length)
    start_fill = jnp.full((segment_length + 1,), marker_index, jnp.int32)
    return start_fill.at[target].set(jnp.arange(present_mask.shape[0], dtype=jnp.int32))[
        :segment_length
    ]


def line_tables(side_len):
    line_coord = jnp.arange(side_len, dtype=jnp.int32) - side_len // 2
    turn_count = line_coord[:, None] * line_coord[None, :] % side_len
    angles = turn_count.astype(jnp.float32) * (TWO_PI / side_len)
    return (jnp.cos(angles), jnp.sin(angles))


def local(
    visibilities,
    tracks,
    freq_ratio,
    blocks_used,
    subgrid_row,
    station_pair,
    subgrid_offsets,
    aterm_screens,
):
    owners = lax.axis_size("sub")
    own_index = lax.axis_index("sub")
    base_count = subgrid_row.shape[0]
    blocks_per = visibilities.shape[2]
    sample_count = visibilities.shape[-1]
    steps_time = tracks.shape[-1] // blocks_per
    pixel_count = aterm_screens.shape[-1]
    capacity = BPP * blocks_per
    slot_indices = owners * capacity
    block_count = base_count * blocks_per
    ratio_row = freq_ratio[0]
    block_vis = visibilities[0].reshape(block_count, 2, sample_count)
    block_tracks = (
        tracks.reshape(base_count, 2, blocks_per, steps_time)
        .transpose(0, 2, 1, 3)
        .reshape(block_count, 2, steps_time)
    )
    used = (jnp.arange(blocks_per, dtype=jnp.int32)[None, :] < blocks_used[:, None]).reshape(
        block_count
    )
    row_of = jnp.repeat(subgrid_row, blocks_per)
    target_owner = row_of // base_count
    onehot_int = (
        (target_owner[:, None] == jnp.arange(owners, dtype=jnp.int32)[None, :]) & used[:, None]
    ).astype(jnp.int32)
    position = jnp.sum((jnp.cumsum(onehot_int, axis=0) - onehot_int) * onehot_int, axis=1)
    send_slot = jnp.where(used, target_owner * capacity + position, slot_indices)
    source = (
        jnp.full((slot_indices + 1,), block_count, jnp.int32)
        .at[send_slot]
        .set(jnp.arange(block_count, dtype=jnp.int32))[:slot_indices]
    )
    filled = source < block_count
    pick_index = jnp.minimum(source, block_count - 1)
    meta_rows = jnp.where(filled, row_of[pick_index], -1)
    meta_pairs = jnp.repeat(station_pair, blocks_per, axis=0)[pick_index]
    block_meta = jnp.concatenate([meta_rows[:, None], meta_pairs], axis=1)
    send_vis = jnp.where(filled[:, None, None], block_vis[pick_index], jnp.zeros((), jnp.bfloat16))
    send_tracks = jnp.where(filled[:, None, None], block_tracks[pick_index], 0.0)
    got_vis, got_meta = (
        lax.all_to_all(send_vis, "sub", split_axis=0, concat_axis=0, tiled=True),
        lax.all_to_all(block_meta, "sub", split_axis=0, concat_axis=0, tiled=True),
    )
    got_tracks = lax.all_to_all(send_tracks, "sub", split_axis=0, concat_axis=0, tiled=True)
    heavy_count = 3 * owners // 4
    receive_most = heavy_count * BPP * blocks_per + (owners - heavy_count) * BPP * 2
    padded_rows = -(-receive_most // 8) * 8
    received_rows = got_meta[:, 0]
    packed_row_order = packing_result(received_rows >= 0, padded_rows, slot_indices)
    use_vis = jnp.take(got_vis, packed_row_order, axis=0, mode="fill", fill_value=0)
    use_tracks = jnp.take(got_tracks, packed_row_order, axis=0, mode="fill", fill_value=0)
    use_rows = jnp.take(received_rows, packed_row_order, axis=0, mode="fill", fill_value=-1)
    local_row = use_rows - own_index * base_count
    centre = lookup(subgrid_offsets, local_row)
    images = blocks_to_images(use_vis, use_tracks, centre, ratio_row)
    selector = (jnp.arange(base_count, dtype=jnp.int32)[:, None] == local_row[None, :]).astype(
        jnp.bfloat16
    )
    summed = jnp.dot(
        selector,
        images.reshape(images.shape[0], 2 * pixel_count),
        preferred_element_type=jnp.float32,
    ).reshape(base_count, 2, pixel_count)
    slot_rows = got_meta[:, 0] - own_index * base_count
    slot_match = jnp.arange(base_count, dtype=jnp.int32)[:, None] == slot_rows[None, :]
    row_station = jnp.max(jnp.where(slot_match[:, :, None], got_meta[None, :, 1:], 0), axis=1)
    piece = lax.all_gather(aterm_screens, "sub", axis=1, tiled=True)
    rows_here = piece.shape[1]
    station_ids = jnp.arange(rows_here, dtype=jnp.int32)
    choose_rows = (row_station[:, :, None] == station_ids[None, None, :]).astype(jnp.bfloat16)
    flat_piece = piece[0].reshape(rows_here, 2 * pixel_count)
    chosen = jnp.einsum("bsj,jx->bsx", choose_rows, flat_piece, preferred_element_type=jnp.float32)
    first_real = chosen[:, 0, :pixel_count]
    first_imag = chosen[:, 0, pixel_count:]
    second_real = chosen[:, 1, :pixel_count]
    second_imag = chosen[:, 1, pixel_count:]
    coords = jnp.arange(SUB, dtype=jnp.float32) - SUB // 2
    taper_line = 1.0 - (2.0 * coords / (SUB + 2)) ** 2
    taper_map = (taper_line[:, None] * taper_line[None, :]).reshape(SUB * SUB)
    tap_real = summed[:, 0] * taper_map
    tap_imag = summed[:, 1] * taper_map
    gain_real = first_real * second_real + first_imag * second_imag
    gain_imag = first_real * second_imag - first_imag * second_real
    weight_real = (tap_real * gain_real - tap_imag * gain_imag).reshape(base_count, SUB, SUB)
    weight_imag = (tap_real * gain_imag + tap_imag * gain_real).reshape(base_count, SUB, SUB)
    cos_line, sin_line = line_tables(SUB)
    highest = lax.Precision.HIGHEST
    half_real = jnp.einsum("bqr,ry->bqy", weight_real, cos_line, precision=highest) + jnp.einsum(
        "bqr,ry->bqy", weight_imag, sin_line, precision=highest
    )
    half_imag = jnp.einsum("bqr,ry->bqy", weight_imag, cos_line, precision=highest) - jnp.einsum(
        "bqr,ry->bqy", weight_real, sin_line, precision=highest
    )
    out_real = jnp.einsum("qx,bqy->bxy", cos_line, half_real, precision=highest) + jnp.einsum(
        "qx,bqy->bxy", sin_line, half_imag, precision=highest
    )
    out_imag = jnp.einsum("qx,bqy->bxy", cos_line, half_imag, precision=highest) - jnp.einsum(
        "qx,bqy->bxy", sin_line, half_real, precision=highest
    )
    out_real = out_real.reshape(base_count, SUB * SUB) / SUB
    out_imag = out_imag.reshape(base_count, SUB * SUB) / SUB
    return jnp.stack([out_real, out_imag], axis=1)[None]


def solution(mesh):
    in_specs = (
        P("chan", ("grp", "sub"), None, None, None),
        P(("grp", "sub"), None, None),
        P(("grp", "chan"), None),
        P(("grp", "sub")),
        P(("grp", "sub")),
        P(("grp", "sub"), None),
        P(("grp", "sub"), None),
        P("chan", ("grp", "sub"), None, None),
    )
    out_specs = P("chan", ("grp", "sub"), None, None)
    return jax.shard_map(local, mesh=mesh, in_specs=in_specs, out_specs=out_specs, check_vma=False)
```

profile of v0, /device:TPU:0, one launch (start us, length us, event | category | flops | bytes accessed | tf_op | source)
XLA Modules:
  0.0 96.5 jit_solution(17183527406381024529)
XLA Ops:
  0.0 0.8 iota_compare_fusion.5
  0.9 0.7 broadcast_in_dim.148
  1.8 0.8 copy.144
  3.2 0.7 scatter_custom_fusion
  3.9 0.7 gather_fusion
  5.4 0.6 copy.114
  6.0 6.3 %all-to-all-start = ((s32[4,8,3]{1,2,0:T(4,128)}), s32[4,8,3]{1,2,0:T(4,128)S(1)}, u32[]{:S(2)}, u32[]{:S(2)}) async-start(s32[4,8,3]{1,2,0:T(4,128)} %copy.114), calls=%async_computation | async-start | bytes 16384 | tf_op jit(solution)/shard_map/all_to_all | solution.py:145
  12.4 0.8 reshape.412
  13.2 0.6 gather_fusion.5
  13.8 0.8 gather_fusion.3
  14.7 0.8 broadcast_select_fusion
  15.6 16.0 %all_gather.3 = bf16[1,128,2,1024]{3,2,0,1:T(2,128)(2,1)S(1)} all-gather(bf16[1,32,2,1024]{3,2,0,1:T(2,128)(2,1)} %bitcast.140), channel_id=1, replica_groups=mesh['grp'=2,'sub'=4,'chan'=4] {'sub'}, dimensions={1}, use_global_device_ids=true | all-gather | bytes 655360 | tf_op jit(solution)/shard_map/all_gather | solution.py:170
  31.6 0.7 reshape.511
  32.7 5.4 %all-to-all-start.2 = ((f32[4,1,256]{2,1,0:T(1,128)}), f32[4,1,256]{2,1,0:T(1,128)S(1)}, u32[]{:S(2)}, u32[]{:S(2)}) async-start(f32[4,1,256]{2,1,0:T(1,128)} %reshape.511), calls=%async_computation.2 | async-start | bytes 8192 | tf_op jit(solution)/shard_map/all_to_all | solution.py:147
  38.5 0.7 scatter_custom_fusion.1
  39.2 0.7 gather_fusion.2
  40.7 2.9 %all-to-all-done.2 = f32[4,1,256]{2,1,0:T(1,128)S(1)} async-done(((f32[4,1,256]{2,1,0:T(1,128)}), f32[4,1,256]{2,1,0:T(1,128)S(1)}, u32[]{:S(2)}, u32[]{:S(2)}) %all-to-all-start.2) | async-done | bytes 4128 | tf_op jit(solution)/shard_map/all_to_all | solution.py:147
  43.7 3.5 %all-to-all-start.1 = ((bf16[32,2,1024]{2,1,0:T(2,128)(2,1)}), bf16[32,2,1024]{2,1,0:T(2,128)(2,1)S(1)}, u32[]{:S(2)}, u32[]{:S(2)}) async-start(bf16[32,2,1024]{2,1,0:T(2,128)(2,1)} %broadcast_select_fusion), calls=%async_computation.1 | async-start | bytes 262144 | tf_op jit(solution)/shard_map/all_to_all | solution.py:144
  47.7 0.7 reduce.5
  48.5 0.6 gather_fusion.6
  49.1 3.7 %all-to-all-done.1 = bf16[32,2,1024]{2,1,0:T(2,128)(2,1)S(1)} async-done(((bf16[32,2,1024]{2,1,0:T(2,128)(2,1)}), bf16[32,2,1024]{2,1,0:T(2,128)(2,1)S(1)}, u32[]{:S(2)}, u32[]{:S(2)}) %all-to-all-start.1) | async-done | bytes 131104 | tf_op jit(solution)/shard_map/all_to_all | solution.py:144
  52.9 0.8 gather_fusion.4
  53.8 38.6 %while.11 = (s32[]{:T(128)}, bf16[4,8,2,1024]{3,1,2,0:T(8,128)(2,1)S(1)}, bf16[4,8,2,1024]{3,1,0,2:T(8,128)(2,1)S(1)}, f32[4,8,2,16]{3,1,0,2:T(8,128)S(1)}, f32[...) while((s32[]{:T(128)}, bf16[4,8,2,1024]{3,1,2,0:T(8,128)(2,1)S(1)}, ...), condition=%wide.region_7.8_spmd.clone, body=%wide.region_6.7_spmd.clone.sunk | while | flops 80642080 | bytes 13520677 | solution.py:60
  54.4 7.3 %multiply_sine_fusion.2 = (f32[8,2,32,1024]{3,2,0,1:T(8,128)S(1)}, f32[8,2,32,1024]{3,2,0,1:T(8,128)S(1)}) fusion(f32[32]{0:T(128)S(1)} %iota_add_fusion.3, f32[8,2,1024]{2,0,1:T(8,128)S(1)} %subtract_multiply_fusion.2), kind=kLoop, calls=%fused_computation.10.clone.1 | loop fusion | flops 524288 | bytes 4259968 | tf_op jit(solution)/shard_map/while/body/eval_jaxpr/sin | solution.py:33
  62.2 0.8 fusion.129
  64.1 7.3 %multiply_sine_fusion.2 = (f32[8,2,32,1024]{3,2,0,1:T(8,128)S(1)}, f32[8,2,32,1024]{3,2,0,1:T(8,128)S(1)}) fusion(f32[32]{0:T(128)S(1)} %iota_add_fusion.3, f32[8,2,1024]{2,0,1:T(8,128)S(1)} %subtract_multiply_fusion.2), kind=kLoop, calls=%fused_computation.10.clone.1 | loop fusion | flops 524288 | bytes 4259968 | tf_op jit(solution)/shard_map/while/body/eval_jaxpr/sin | solution.py:33
  71.9 0.8 fusion.129
  73.7 7.3 %multiply_sine_fusion.2 = (f32[8,2,32,1024]{3,2,0,1:T(8,128)S(1)}, f32[8,2,32,1024]{3,2,0,1:T(8,128)S(1)}) fusion(f32[32]{0:T(128)S(1)} %iota_add_fusion.3, f32[8,2,1024]{2,0,1:T(8,128)S(1)} %subtract_multiply_fusion.2), kind=kLoop, calls=%fused_computation.10.clone.1 | loop fusion | flops 524288 | bytes 4259968 | tf_op jit(solution)/shard_map/while/body/eval_jaxpr/sin | solution.py:33
  81.5 0.8 fusion.129
  83.3 7.3 %multiply_sine_fusion.2 = (f32[8,2,32,1024]{3,2,0,1:T(8,128)S(1)}, f32[8,2,32,1024]{3,2,0,1:T(8,128)S(1)}) fusion(f32[32]{0:T(128)S(1)} %iota_add_fusion.3, f32[8,2,1024]{2,0,1:T(8,128)S(1)} %subtract_multiply_fusion.2), kind=kLoop, calls=%fused_computation.10.clone.1 | loop fusion | flops 524288 | bytes 4259968 | tf_op jit(solution)/shard_map/while/body/eval_jaxpr/sin | solution.py:33
  91.1 0.8 fusion.129
  95.9 0.6 copy.133
  (150 shorter events, 13.4 us)
Async XLA Ops:
  0.0 13.8 %copy-start = (bf16[1,4,8,2,1024]{4,3,2,1,0:T(2,128)(2,1)S(1)}, bf16[1,4,8,2,1024]{4,3,2,1,0:T(2,128)(2,1)}, u32[]{:S(2)}) copy-start(bf16[1,4,8,2,1024]{4,3,2,1,0:T(2,128)(2,1)} %param.10) | copy-start | bytes 393220
  4.6 35.8 %copy-start.2 = (s32[4,2]{0,1:T(2,128)S(1)}, s32[4,2]{0,1:T(2,128)}, u32[]{:S(2)}) copy-start(s32[4,2]{0,1:T(2,128)} %param.16) | copy-start | bytes 100
  6.0 26.7 %all-to-all-start = ((s32[4,8,3]{1,2,0:T(4,128)}), s32[4,8,3]{1,2,0:T(4,128)S(1)}, u32[]{:S(2)}, u32[]{:S(2)}) async-start(s32[4,8,3]{1,2,0:T(4,128)} %copy.114), calls=%async_computation | async-start | bytes 16384 | tf_op jit(solution)/shard_map/all_to_all | solution.py:145
  15.6 38.2 %copy-start.1 = (f32[1,64]{1,0:T(1,128)S(1)}, f32[1,64]{1,0:T(1,128)}, u32[]{:S(2)}) copy-start(f32[1,64]{1,0:T(1,128)} %param.12) | copy-start | bytes 772
  32.7 11.0 %all-to-all-start.2 = ((f32[4,1,256]{2,1,0:T(1,128)}), f32[4,1,256]{2,1,0:T(1,128)S(1)}, u32[]{:S(2)}, u32[]{:S(2)}) async-start(f32[4,1,256]{2,1,0:T(1,128)} %reshape.511), calls=%async_computation.2 | async-start | bytes 8192 | tf_op jit(solution)/shard_map/all_to_all | solution.py:147
  43.7 9.2 %all-to-all-start.1 = ((bf16[32,2,1024]{2,1,0:T(2,128)(2,1)}), bf16[32,2,1024]{2,1,0:T(2,128)(2,1)S(1)}, u32[]{:S(2)}, u32[]{:S(2)}) async-start(bf16[32,2,1024]{2,1,0:T(2,128)(2,1)} %broadcast_select_fusion), calls=%async_computation.1 | async-start | bytes 262144 | tf_op jit(solution)/shard_map/all_to_all | solution.py:144
where the time goes:
time: 96.9 us; the launch traced here: 96.5 us
  other arithmetic  35.3 us (36%)
  local copies, waits for them, and re-layouts  16.3 us (17%)
  blocking collectives  16 us (17%)
  starting transfers between devices  15.2 us (16%)
  waiting for transfers between devices  6.64 us (7%)
  matrix products  6.36 us (7%)
    sin x4, other arithmetic, one_group(): sine_table = jnp.sin(angles)  29.2 us
    all_gather x1, blocking collectives, local(): piece = lax.all_gather(aterm_screens, 'sub', axis=1, tiled=True)  16 us
    all_to_all x1, starting transfers between devices, local(): lax.all_to_all(block_meta, 'sub', split_axis=0, concat_axis=0, tiled=True)  6.32 us
    all_to_all x1, starting transfers between devices, local(): lax.all_to_all(send_tracks, 'sub', split_axis=0, concat_axis=0, tiled=True)  5.4 us
    all_to_all x1, waiting for transfers between devices, local(): lax.all_to_all(send_vis, 'sub', split_axis=0, concat_axis=0, tiled=True)  3.73 us
    all_to_all x1, starting transfers between devices, local(): lax.all_to_all(send_vis, 'sub', split_axis=0, concat_axis=0, tiled=True)  3.5 us
    dot_general x4, matrix products, one_group(): jnp.einsum('glk,gnk->gln', left_side, right_side, preferred_element_type=...  3.29 us
    all_to_all x1, waiting for transfers between devices, local(): lax.all_to_all(send_tracks, 'sub', split_axis=0, concat_axis=0, tiled=True)  2.91 us
  transfers between devices with their start and end apart: 3, of which 2 were waited for; matrix products, arithmetic and copies ran while one was open for 9% of the time, Pallas kernels for 0%

commit v1 on v0

v1 whole, which is shorter than its diff:
```python
import functools
import math

import jax
import jax.numpy as jnp
from jax import lax
from jax.experimental import pallas as pl
from jax.experimental.pallas import tpu as pltpu
from jax.sharding import PartitionSpec as P

SUB = 32
LANES = 128
SLOTS = LANES // SUB
QROWS = SUB // SLOTS
META = 16
TWO_PI = 2.0 * math.pi
HIGHEST = lax.Precision.HIGHEST


def turn_cos_sin(turns):
    part = turns - jnp.round(turns)
    square = part * part
    sine = part * (
        3.14159264 + square * (-5.16771008 + square * (2.55007752 + square * (-0.59829129 + square * 0.07765766)))
    )
    cosine = 0.99999995 + square * (
        -4.93479283 + square * (4.05841135 + square * (-1.33187657 + square * 0.21968961))
    )
    return 1.0 - 2.0 * sine * sine, 2.0 * sine * cosine


def times(a_real, a_imag, b_real, b_imag):
    return a_real * b_real - a_imag * b_imag, a_real * b_imag + a_imag * b_real


def iota(shape, axis):
    return lax.broadcasted_iota(jnp.int32, shape, axis)


def image_kernel(axis_size, used_ref, row_ref, pair_ref, vis_ref, tracks_ref, freq_ref, *rest):
    send_refs, (lines_ref, turns_ref, powers_ref, total_ref) = rest[:-4], rest[-4:]
    base_count, blocks, _, samples = vis_ref.shape[1:]
    channels = freq_ref.shape[1]
    steps = samples // channels
    me = lax.axis_index("sub")
    lines = 2 * base_count

    for b in range(base_count):
        lines_ref[2 * b : 2 * b + 2, :] = tracks_ref[b]
    spread = (iota((channels, samples), 1) // steps == iota((channels, samples), 0)).astype(jnp.float32)
    ratio = jnp.dot(
        jnp.broadcast_to(freq_ref[...], (8, channels)), spread, precision=HIGHEST, preferred_element_type=jnp.float32
    )[0:1]
    most = used_ref[0]
    for b in range(1, base_count):
        most = jnp.maximum(most, used_ref[b])

    def prepare(j, _):
        pick = iota((blocks * steps, samples), 0) == j * steps + iota((blocks * steps, samples), 1) % steps
        moved = jnp.dot(
            lines_ref[...], pick.astype(jnp.float32), precision=HIGHEST, preferred_element_type=jnp.float32
        )
        turns = moved * ratio * (1.0 / SUB)
        turns = turns - jnp.round(turns)
        turns_ref[j] = turns
        weight = jnp.where(iota((lines, 1), 0) % 2 == 0, 1.0, float(QROWS))
        one = turn_cos_sin(turns * weight)
        two = times(*one, *one)
        three = times(*two, *one)
        for power, (real, imag) in enumerate((one, two, three)):
            powers_ref[j, 2 * power] = real
            powers_ref[j, 2 * power + 1] = imag
        return 0

    lax.fori_loop(0, most, prepare, 0)
    total_ref[...] = jnp.zeros_like(total_ref)
    q_start = (iota((QROWS, 1), 0) * SLOTS - SUB // 2).astype(jnp.float32)
    r_start = (iota((QROWS, 1), 0) - SUB // 2).astype(jnp.float32)
    for b in range(base_count):

        def one_block(j, sums):
            sample = vis_ref[0, b, j].astype(jnp.float32)

            def fan(real, imag, line):
                reals, imags = [real], [imag]
                for power in range(SLOTS - 1):
                    power_real = powers_ref[j, 2 * power, line : line + 1, :]
                    power_imag = powers_ref[j, 2 * power + 1, line : line + 1, :]
                    next_real, next_imag = times(real, imag, power_real, power_imag)
                    reals.append(next_real)
                    imags.append(next_imag)
                return jnp.concatenate(reals + imags, axis=0).astype(jnp.bfloat16)

            base = turn_cos_sin(turns_ref[j, 2 * b : 2 * b + 1, :] * q_start)
            left = fan(*times(*base, sample[0:1], sample[1:2]), 2 * b)
            right = fan(*turn_cos_sin(turns_ref[j, 2 * b + 1 : 2 * b + 2, :] * r_start), 2 * b + 1)
            return sums + lax.dot_general(left, right, (((1,), (1,)), ((), ())), preferred_element_type=jnp.float32)

        sums = lax.fori_loop(0, used_ref[b], one_block, jnp.zeros((2 * SUB, 2 * SUB), jnp.float32))
        real = sums[:SUB, :SUB] - sums[SUB:, SUB:]
        imag = sums[:SUB, SUB:] + sums[SUB:, :SUB]
        image = jnp.concatenate([real, imag], axis=0) * samples**-0.5
        stations = iota((META, SUB), 0)
        stations = jnp.where(stations == 0, pair_ref[b, 0], jnp.where(stations == 1, pair_ref[b, 1], 0))
        image = jnp.concatenate([image, stations.astype(jnp.float32)], axis=0)
        image = jnp.concatenate([image, jnp.zeros((image.shape[0], LANES - SUB), jnp.float32)], axis=1)
        row = row_ref[b]
        owner = row // base_count
        slot = row % base_count
        place = lax.rem(owner - me + axis_size, axis_size)
        image = pltpu.roll(image, (slot % SLOTS) * SUB, 1)
        total_ref[place, slot // SLOTS] += image
    if len(send_refs) == 1:
        send_refs[0][...] = total_ref[...].astype(jnp.bfloat16)
    else:
        for place, send_ref in enumerate(send_refs):
            send_ref[...] = total_ref[place].astype(jnp.bfloat16)


def gather_kernel(offset_ref, *rest):
    payload_refs, (pixels_ref, station_ref) = rest[:-2], rest[-2:]
    groups = pixels_ref.shape[0] // SLOTS
    for g in range(groups):
        parts = []
        for ref in payload_refs:
            parts += [ref[g]] if len(ref.shape) == 3 else [ref[p, g] for p in range(ref.shape[0])]
        whole = parts[0].astype(jnp.float32)
        for part in parts[1:]:
            whole = whole + part.astype(jnp.float32)
        lane = iota((QROWS, LANES), 1)
        q = iota((QROWS, LANES), 0) * SLOTS + lane // SUB - SUB // 2
        r = lane % SUB - SUB // 2
        line = lambda h: 1.0 - (2.0 * h.astype(jnp.float32) / (SUB + 2)) ** 2
        taper = line(q) * line(r)
        names = whole[2 * SUB : 2 * SUB + 8].astype(jnp.int32)
        for s in range(SLOTS):
            slot = g * SLOTS + s
            flat = []
            for c in range(2):
                value = jnp.zeros((QROWS, LANES), jnp.float32)
                for i in range(SLOTS):
                    start = c * SUB + i * QROWS
                    moved = pltpu.roll(whole[start : start + QROWS], ((i - s) % SLOTS) * SUB, 1)
                    value = jnp.where(lane // SUB == i, moved, value)
                flat.append(value)
            turn = lax.rem(offset_ref[slot, 0] * q + offset_ref[slot, 1] * r, SUB)
            cosine, sine = turn_cos_sin(turn.astype(jnp.float32) * (1.0 / SUB))
            real, imag = times(*flat, cosine * taper, -sine * taper)
            pixels_ref[slot, 0] = real
            pixels_ref[slot, 1] = imag
            for e in range(2):
                station_ref[slot, e] = names[e, s * SUB]


def finish_kernel(station_ref, pixels_ref, screens_ref, out_ref, picked_ref, rows_ref, sems):
    base_count = pixels_ref.shape[0]
    copies = []
    for n in range(2 * base_count):
        copy = pltpu.make_async_copy(
            screens_ref.at[0, station_ref[n // 2, n % 2]], picked_ref.at[n], sems.at[n]
        )
        copy.start()
        copies.append(copy)
    order = lambda n: (n % QROWS) * SLOTS + n // QROWS - SUB // 2
    size = (LANES, LANES)
    same = iota(size, 0) // SUB == iota(size, 1) // SUB
    turn = (iota(size, 0) % SUB - SUB // 2) * (iota(size, 1) % SUB - SUB // 2)
    r_cos, r_sin = turn_cos_sin(turn.astype(jnp.float32) * (1.0 / SUB))
    r_table = jnp.concatenate([jnp.where(same, r_cos, 0.0), jnp.where(same, r_sin, 0.0)], axis=1)
    size = (SUB, SUB)
    q_cos, q_sin = turn_cos_sin((order(iota(size, 0)) * order(iota(size, 1))).astype(jnp.float32) * (1.0 / SUB))
    q_table = jnp.concatenate(
        [jnp.concatenate([q_cos, q_sin], axis=1), jnp.concatenate([-q_sin, q_cos], axis=1)], axis=0
    ) * (1.0 / SUB)
    lane = iota((QROWS, LANES), 1)
    for copy in copies:
        copy.wait()
    for g in range(base_count // SLOTS):
        weighted = []
        for s in range(SLOTS):
            slot = g * SLOTS + s
            screens = []
            for e in range(2):
                n = 2 * slot + e
                value = picked_ref[n].astype(jnp.float32)
                for a in range(QROWS):
                    rows_ref[n, 2 * a : 2 * a + 2, :] = value[:, a * LANES : (a + 1) * LANES]
                screens.append((rows_ref[n, pl.ds(0, QROWS, stride=2), :], rows_ref[n, pl.ds(1, QROWS, stride=2), :]))
            (p_real, p_imag), (s_real, s_imag) = screens
            gain = times(p_real, -p_imag, s_real, s_imag)
            weighted.append(times(pixels_ref[slot, 0], pixels_ref[slot, 1], *gain))
        planes = []
        for c in range(2):
            for i in range(SLOTS):
                value = jnp.zeros((QROWS, LANES), jnp.float32)
                for s in range(SLOTS):
                    moved = pltpu.roll(weighted[s][c], ((s - i) % SLOTS) * SUB, 1)
                    value = jnp.where(lane // SUB == s, moved, value)
                planes.append(value)
        planes = jnp.concatenate(planes, axis=0)
        half = jnp.dot(planes, r_table, precision=HIGHEST, preferred_element_type=jnp.float32)
        half_real = half[:SUB, :LANES] + half[SUB:, LANES:]
        half_imag = half[SUB:, :LANES] - half[:SUB, LANES:]
        half = jnp.concatenate([half_real, half_imag], axis=0)
        full = jnp.dot(q_table, half, precision=HIGHEST, preferred_element_type=jnp.float32)
        for s in range(SLOTS):
            for c in range(2):
                value = jnp.zeros((QROWS, LANES), jnp.float32)
                for i in range(SLOTS):
                    start = c * SUB + i * QROWS
                    moved = pltpu.roll(full[start : start + QROWS], ((i - s) % SLOTS) * SUB, 1)
                    value = jnp.where(lane // SUB == i, moved, value)
                for a in range(QROWS):
                    out_ref[0, g * SLOTS + s, c : c + 1, a * LANES : (a + 1) * LANES] = value[a : a + 1]


def local(
    visibilities, tracks, freq_ratio, blocks_used, subgrid_row, station_pair, subgrid_offsets, aterm_screens
):
    owners = lax.axis_size("sub")
    base_count, blocks, _, samples = visibilities.shape[1:]
    groups = -(-base_count // SLOTS)
    pixels = aterm_screens.shape[-1]
    rows = 2 * SUB + META
    vmem = pl.BlockSpec(memory_space=pltpu.VMEM)
    smem = pl.BlockSpec(memory_space=pltpu.SMEM)
    screens = lax.all_gather(aterm_screens, "sub", axis=1, tiled=True)
    direct = owners <= 8
    if direct:
        sends = [jax.ShapeDtypeStruct((groups, rows, LANES), jnp.bfloat16)] * owners
    else:
        sends = [jax.ShapeDtypeStruct((owners, groups, rows, LANES), jnp.bfloat16)]
    sent = pl.pallas_call(
        functools.partial(image_kernel, owners),
        out_shape=sends,
        in_specs=[smem, smem, smem, vmem, vmem, vmem],
        out_specs=[vmem] * len(sends),
        scratch_shapes=[
            pltpu.VMEM((2 * base_count, tracks.shape[-1]), jnp.float32),
            pltpu.VMEM((blocks, 2 * base_count, samples), jnp.float32),
            pltpu.VMEM((blocks, 2 * (SLOTS - 1), 2 * base_count, samples), jnp.float32),
            pltpu.VMEM((owners, groups, rows, LANES), jnp.float32),
        ],
        compiler_params=pltpu.CompilerParams(vmem_limit_bytes=48 * 1024 * 1024),
        name="images",
    )(blocks_used, subgrid_row, station_pair, visibilities, tracks, freq_ratio)
    if direct:
        payloads = [sent[0]]
        for shift in range(1, owners):
            payloads.append(lax.ppermute(sent[shift], "sub", [(n, (n + shift) % owners) for n in range(owners)]))
    else:
        here = lax.axis_index("sub")
        payloads = [lax.all_to_all(jnp.roll(sent[0], here, axis=0), "sub", 0, 0, tiled=True)]
    subgrids, stations = pl.pallas_call(
        gather_kernel,
        out_shape=[
            jax.ShapeDtypeStruct((base_count, 2, QROWS, LANES), jnp.float32),
            jax.ShapeDtypeStruct((base_count, 2), jnp.int32),
        ],
        in_specs=[smem] + [vmem] * len(payloads),
        out_specs=[vmem, smem],
        compiler_params=pltpu.CompilerParams(vmem_limit_bytes=48 * 1024 * 1024),
        name="subgrids",
    )(subgrid_offsets, *payloads)
    return pl.pallas_call(
        finish_kernel,
        out_shape=jax.ShapeDtypeStruct((1, base_count, 2, pixels), jnp.float32),
        in_specs=[smem, vmem, pl.BlockSpec(memory_space=pl.ANY)],
        out_specs=vmem,
        scratch_shapes=[
            pltpu.VMEM((2 * base_count, 2, pixels), jnp.bfloat16),
            pltpu.VMEM((2 * base_count, 2 * QROWS, LANES), jnp.float32),
            pltpu.SemaphoreType.DMA((2 * base_count,)),
        ],
        compiler_params=pltpu.CompilerParams(vmem_limit_bytes=48 * 1024 * 1024),
        name="finish",
    )(stations, subgrids, screens)


def solution(mesh):
    in_specs = (
        P("chan", ("grp", "sub"), None, None, None),
        P(("grp", "sub"), None, None),
        P(("grp", "chan"), None),
        P(("grp", "sub")),
        P(("grp", "sub")),
        P(("grp", "sub"), None),
        P(("grp", "sub"), None),
        P("chan", ("grp", "sub"), None, None),
    )
    out_specs = P("chan", ("grp", "sub"), None, None)
    return jax.shard_map(local, mesh=mesh, in_specs=in_specs, out_specs=out_specs, check_vma=False)
```

time: 96.9 us -> 37.8 us (0.39)
  other arithmetic: 35.3 us -> 0 us
  local copies, waits for them, and re-layouts: 16.3 us -> 2.5 us
  Pallas kernels: 0 us -> 12.8 us
  starting transfers between devices: 15.2 us -> 7.01 us
  waiting for transfers between devices: 6.64 us -> 0.01 us
  matrix products: 6.36 us -> 0 us
    sin x4 -> x0, other arithmetic: 29.2 us -> none  [one_group(): sine_table = jnp.sin(angles)]
    all_to_all x3 -> x0, starting transfers between devices: 15.2 us -> none  [the longest x1 6.32 us: local(): lax.all_to_all(block_meta, 'sub', split_axis=0, concat_axis=0, tiled=True)]
    pallas_call x0 -> x3, Pallas kernels: none -> 12.8 us  [the longest x1 9.42 us: local(): pl.pallas_call(functools.partial(image_kernel, owners), out_shape=sends,...]
    ppermute x0 -> x3, starting transfers between devices: none -> 7.01 us  [local(): lax.ppermute(sent[shift], 'sub', [(n, (n + shift) % owners) for n in rang...]
    all_to_all x3 -> x0, waiting for transfers between devices: 6.64 us -> none  [the longest x1 3.73 us: local(): lax.all_to_all(send_vis, 'sub', split_axis=0, concat_axis=0, tiled=True)]
    dot_general x14 -> x0, matrix products: 6.36 us -> none  [the longest x4 3.29 us: one_group(): jnp.einsum('glk,gnk->gln', left_side, right_side, preferred_element_type=...]
    gather x7 -> x0, local copies, waits for them, and re-layouts: 4.83 us -> none  [the longest x1 0.82 us: local(): block_vis[pick_index]]
    mul x20 -> x0, local copies, waits for them, and re-layouts: 1.86 us -> none  [one_group(): group_tracks[:, :, None, :] * ratio_row[None, None, :, None]]
  transfers between devices with their start and end apart: 3 -> 3, of which waited for: 2 -> 0; matrix products, arithmetic and copies ran while one was open for 9% -> 0% of each run, Pallas kernels for 0% -> 0%
where the time goes in v1:
time: 37.8 us; the launch traced here: 38.3 us
  blocking collectives  15.9 us (42%)
  Pallas kernels  12.8 us (34%)
  starting transfers between devices  7.01 us (19%)
  local copies, waits for them, and re-layouts  2.5 us (7%)
    all_gather x1, blocking collectives, local(): screens = lax.all_gather(aterm_screens, 'sub', axis=1, tiled=True)  15.9 us
    pallas_call x1, Pallas kernels, local(): pl.pallas_call(functools.partial(image_kernel, owners), out_shape=sends,...  9.42 us
    ppermute x3, starting transfers between devices, local(): lax.ppermute(sent[shift], 'sub', [(n, (n + shift) % owners) for n in rang...  7.01 us
    unnamed x16, local copies, waits for them, and re-layouts  2.5 us
    pallas_call x1, Pallas kernels, local(): pl.pallas_call(finish_kernel, out_shape=jax.ShapeDtypeStruct((1, base_cou...  2.08 us
    pallas_call x1, Pallas kernels, local(): pl.pallas_call(gather_kernel, out_shape=[jax.ShapeDtypeStruct((base_count...  1.3 us
  transfers between devices with their start and end apart: 3, of which 0 were waited for; matrix products, arithmetic and copies ran while one was open for 0% of the time, Pallas kernels for 0%

profile of v1, /device:TPU:0, one launch (start us, length us, event | category | flops | bytes accessed | tf_op | source)
XLA Modules:
  0.0 38.3 jit_solution(1217532676070901295)
XLA Ops:
  0.0 0.0 copy-start.3
  0.0 0.0 copy-start.2
  0.0 0.0 copy-start.4
  0.0 0.8 %copy.11.pair_ref = s32[4,2]{1,0:T(4,128)S(1)} copy(s32[4,2]{0,1:T(2,128)} %param.13) | data formatting | bytes 64 | tf_op args[5]
  0.8 0.0 copy-done.3
  0.8 0.0 copy-done.2
  0.8 0.0 copy-done.4
  0.8 0.0 copy-start
  0.8 0.9 %copy-done = bf16[1,4,8,2,1024]{4,3,2,1,0:T(2,128)(2,1)S(1)} copy-done((bf16[1,4,8,2,1024]{4,3,2,1,0:T(2,128)(2,1)S(1)}, bf16[1,4,8,2,1024]{4,3,2,1,0:T(2,128)(2,1)}, u32[]{:S(2)}) %copy-start) | copy-done | bytes 131096
  1.7 0.0 copy-start.1
  1.7 0.7 %copy-done.1 = f32[4,2,128]{2,1,0:T(2,128)S(1)} copy-done((f32[4,2,128]{2,1,0:T(2,128)S(1)}, f32[4,2,128]{2,1,0:T(2,128)}, u32[]{:S(2)}) %copy-start.1) | copy-done | bytes 4120
  2.4 0.0 copy-start.5
  2.4 9.4 %images.1 = (bf16[1,80,128]{2,1,0:T(8,128)(2,1)S(1)}, bf16[1,80,128]{2,1,0:T(8,128)(2,1)S(1)}, bf16[1,80,128]{2,1,0:T(8,128)(2,1)S(1)}, bf16[1,80,128]{2,1,0:T(8,128)(2,1)S(1)}) custom-call(s32[4]{0:T(128)S(1)} %copy-done.2, s32[4]{0:T(128)S(1)} %copy-done.3, s32[4,2]{1,0:T(4,128)S(1)} %copy.11.pair_ref, bf16[1,4,8,2,1024]{4,3,2,1,0:T(2,128)(2,1)S(1)} %copy-done, ...), custom_call_target="tpu_custom_call" | custom-call | tf_op jit(solution)/shard_map/images/pallas_call | solution.py:233
  11.8 0.1 collective-permute-start
  11.9 5.6 %collective-permute-start.1 = (bf16[1,80,128]{2,1,0:T(8,128)(2,1)S(1)}, bf16[1,80,128]{2,1,0:T(8,128)(2,1)S(1)}, u32[]{:S(2)}, u32[]{:S(2)}) collective-permute-start(bf16[1,80,128]{2,1,0:T(8,128)(2,1)S(1)} %get-tuple-element.13), channel_id=1, source_target_pairs={{0,8},{4,12},{8,0},{12,4},{1,9},{5,13},{9,1},{13,5},{2,10},{6,14},... | collective-permute-start | bytes 61448 | tf_op jit(solution)/shard_map/ppermute | solution.py:250
  17.5 1.3 %collective-permute-start.2 = (bf16[1,80,128]{2,1,0:T(8,128)(2,1)S(1)}, bf16[1,80,128]{2,1,0:T(8,128)(2,1)S(1)}, u32[]{:S(2)}, u32[]{:S(2)}) collective-permute-start(bf16[1,80,128]{2,1,0:T(8,128)(2,1)S(1)} %get-tuple-element.14), channel_id=1, source_target_pairs={{0,12},{4,0},{8,4},{12,8},{1,13},{5,1},{9,5},{13,9},{2,14},{6,2},{... | collective-permute-start | bytes 61448 | tf_op jit(solution)/shard_map/ppermute | solution.py:250
  18.9 0.0 copy-done.5
  18.9 0.0 copy-start.6
  18.9 15.9 %all_gather.3 = bf16[1,128,2,1024]{3,2,0,1:T(2,128)(2,1)S(1)} all-gather(bf16[1,32,2,1024]{3,2,0,1:T(2,128)(2,1)S(1)} %bitcast.3), channel_id=1, replica_groups=mesh['grp'=2,'sub'=4,'chan'=4] {'sub'}, dimensions={1}, use_global_device_ids=true | all-gather | bytes 655360 | tf_op jit(solution)/shard_map/all_gather | solution.py:227
  34.8 0.0 copy-done.6
  34.8 0.1 copy.12.offset_ref
  34.9 0.0 collective-permute-done.rest_1_
  34.9 0.0 collective-permute-done.1.rest_2_
  34.9 0.0 collective-permute-done.2.rest_3_
  34.9 1.3 %subgrids.1 = (f32[4,2,8,128]{3,2,1,0:T(8,128)S(1)}, s32[4,2]{1,0:T(4,128)S(1)}) custom-call(s32[4,2]{1,0:T(4,128)S(1)} %copy.12.offset_ref, bf16[1,80,128]{2,1,0:T(8,128)(2,1)S(1)} %get-tuple-element.11.rest_0_, bf16[1,80,128]{2,1,0:T(8,128)(2,1)S(1)} %collective-permute-done.rest_1_, bf16[1,80,128]{2,1,0:T(8,128)(2,1)S(1)} %collective-permute-done.1.rest_2_, ...), custom_call_target="tpu_custom_call" | custom-call | tf_op jit(solution)/shard_map/subgrids/pallas_call | solution.py:254
  36.2 2.1 %finish.1 = f32[1,4,2,1024]{3,2,1,0:T(2,128)} custom-call(s32[4,2]{1,0:T(4,128)S(1)} %get-tuple-element.15.station_ref, f32[4,2,8,128]{3,2,1,0:T(8,128)S(1)} %get-tuple-element.16.pixels_ref, bf16[1,128,2,1024]{3,2,1,0:T(2,128)(2,1)S(1)} %bitcast.2), custom_call_target="tpu_custom_call" | custom-call | tf_op jit(solution)/shard_map/finish/pallas_call | solution.py:265
Async XLA Ops:
  0.0 0.8 %copy-start.3 = (s32[4]{0:T(128)S(1)}, s32[4]{0:T(128)}, u32[]{:S(2)}) copy-start(s32[4]{0:T(128)} %row_ref.1) | copy-start | bytes 52
  0.0 0.8 %copy-start.2 = (s32[4]{0:T(128)S(1)}, s32[4]{0:T(128)}, u32[]{:S(2)}) copy-start(s32[4]{0:T(128)} %used_ref.1) | copy-start | bytes 52
  0.0 0.8 %copy-start.4 = (f32[1,64]{1,0:T(1,128)S(1)}, f32[1,64]{1,0:T(1,128)}, u32[]{:S(2)}) copy-start(f32[1,64]{1,0:T(1,128)} %freq_ref.1) | copy-start | bytes 772
  0.8 0.9 %copy-start = (bf16[1,4,8,2,1024]{4,3,2,1,0:T(2,128)(2,1)S(1)}, bf16[1,4,8,2,1024]{4,3,2,1,0:T(2,128)(2,1)}, u32[]{:S(2)}) copy-start(bf16[1,4,8,2,1024]{4,3,2,1,0:T(2,128)(2,1)} %vis_ref.1) | copy-start | bytes 393220
  1.7 0.7 %copy-start.1 = (f32[4,2,128]{2,1,0:T(2,128)S(1)}, f32[4,2,128]{2,1,0:T(2,128)}, u32[]{:S(2)}) copy-start(f32[4,2,128]{2,1,0:T(2,128)} %tracks_ref.1) | copy-start | bytes 12292
  2.4 16.4 %copy-start.5 = (bf16[1,32,2,1024]{3,2,1,0:T(2,128)(2,1)S(1)}, bf16[1,32,2,1024]{3,2,1,0:T(2,128)(2,1)}, u32[]{:S(2)}) copy-start(bf16[1,32,2,1024]{3,2,1,0:T(2,128)(2,1)} %param.15) | copy-start | bytes 393220
  11.8 23.1 %collective-permute-start = (bf16[1,80,128]{2,1,0:T(8,128)(2,1)S(1)}, bf16[1,80,128]{2,1,0:T(8,128)(2,1)S(1)}, u32[]{:S(2)}, u32[]{:S(2)}) collective-permute-start(bf16[1,80,128]{2,1,0:T(8,128)(2,1)S(1)} %get-tuple-element.12), channel_id=1, source_target_pairs={{0,4},{4,8},{8,12},{12,0},{1,5},{5,9},{9,13},{13,1},{2,6},{6,10},{... | collective-permute-start | bytes 61448 | tf_op jit(solution)/shard_map/ppermute | solution.py:250
  11.9 23.0 %collective-permute-start.1 = (bf16[1,80,128]{2,1,0:T(8,128)(2,1)S(1)}, bf16[1,80,128]{2,1,0:T(8,128)(2,1)S(1)}, u32[]{:S(2)}, u32[]{:S(2)}) collective-permute-start(bf16[1,80,128]{2,1,0:T(8,128)(2,1)S(1)} %get-tuple-element.13), channel_id=1, source_target_pairs={{0,8},{4,12},{8,0},{12,4},{1,9},{5,13},{9,1},{13,5},{2,10},{6,14},... | collective-permute-start | bytes 61448 | tf_op jit(solution)/shard_map/ppermute | solution.py:250
  17.5 17.4 %collective-permute-start.2 = (bf16[1,80,128]{2,1,0:T(8,128)(2,1)S(1)}, bf16[1,80,128]{2,1,0:T(8,128)(2,1)S(1)}, u32[]{:S(2)}, u32[]{:S(2)}) collective-permute-start(bf16[1,80,128]{2,1,0:T(8,128)(2,1)S(1)} %get-tuple-element.14), channel_id=1, source_target_pairs={{0,12},{4,0},{8,4},{12,8},{1,13},{5,1},{9,5},{13,9},{2,14},{6,2},{... | collective-permute-start | bytes 61448 | tf_op jit(solution)/shard_map/ppermute | solution.py:250
  18.9 15.9 %copy-start.6 = (s32[4,2]{0,1:T(2,128)S(1)}, s32[4,2]{0,1:T(2,128)}, u32[]{:S(2)}) copy-start(s32[4,2]{0,1:T(2,128)} %param.14) | copy-start | bytes 100

commit v2 on v1

v2 whole, which is shorter than its diff:
```python
import functools
import math

import jax
import jax.numpy as jnp
from jax import lax
from jax.experimental import pallas as pl
from jax.experimental.pallas import tpu as pltpu
from jax.sharding import PartitionSpec as P

SUB = 32
LANES = 128
SLOTS = LANES // SUB
QROWS = SUB // SLOTS
ROWS = 2 * SUB + 16
HIGHEST = lax.Precision.HIGHEST
SINE = (3.14159027, -5.16740673, 2.54401052, -0.55946246)
COSINE = (0.99999325, -4.93393467, 4.0412481, -1.22203176)
SINE_LONG = (3.14159264, -5.16771008, 2.55007752, -0.59829129, 0.07765766)
COSINE_LONG = (0.99999995, -4.93479283, 4.05841135, -1.33187657, 0.21968961)


def series(terms, square):
    value = terms[-1]
    for term in terms[-2::-1]:
        value = term + square * value
    return value


def turn_cos_sin(turns, sine_terms=SINE_LONG, cosine_terms=COSINE_LONG):
    part = turns - jnp.round(turns)
    square = part * part
    sine = part * series(sine_terms, square)
    twice = sine + sine
    return 1.0 - twice * sine, twice * series(cosine_terms, square)


def times(a_real, a_imag, b_real, b_imag):
    return a_real * b_real - a_imag * b_imag, a_real * b_imag + a_imag * b_real


def iota(shape, axis):
    return lax.broadcasted_iota(jnp.int32, shape, axis)


def image_kernel(
    axis_size, used_hbm, row_hbm, pair_hbm, vis_hbm, tracks_hbm, freq_hbm, *rest
):
    send_refs, scratch = rest[:-13], rest[-13:]
    (used_ref, row_ref, pair_ref, vis_ref, tracks_ref, freq_ref, lines_ref, turns_ref, powers_ref, total_ref,
     sems, wide_ref, image_ref) = scratch
    base_count, blocks, _, samples = vis_ref.shape
    channels = freq_ref.shape[1]
    steps = samples // channels
    groups = -(-base_count // SLOTS)
    me = lax.axis_index("sub")
    lines = 2 * base_count
    tiles = samples // LANES
    sources = (
        (tracks_hbm, tracks_ref), (freq_hbm, freq_ref), (used_hbm, used_ref), (vis_hbm.at[0], vis_ref),
        (row_hbm, row_ref), (pair_hbm, pair_ref),
    )
    copies = [pltpu.make_async_copy(one, two, sems.at[n]) for n, (one, two) in enumerate(sources)]
    for copy in copies:
        copy.start()
    copies[0].wait()
    copies[1].wait()
    for b in range(base_count):
        lines_ref[2 * b : 2 * b + 2, :] = tracks_ref[b]
    wide_ref[...] = jnp.zeros_like(wide_ref)
    wide_ref[0:1, :channels] = freq_ref[...]
    wide = jnp.broadcast_to(wide_ref[0:1, :], (8, LANES))
    lane = iota((8, LANES), 1)
    ratio = jnp.concatenate(
        [jnp.take_along_axis(wide, (lane + m * LANES) // steps, axis=1) for m in range(tiles)], axis=1
    )[0:1] * (1.0 / SUB)
    weight = jnp.where(iota((lines, 1), 0) % 2 == 0, 1.0, float(QROWS))

    def prepare(j, _):
        moved = jnp.take_along_axis(lines_ref[...], iota((lines, LANES), 1) % steps + j * steps, axis=1)
        turns = jnp.concatenate([moved] * tiles, axis=1) * ratio
        turns = turns - jnp.round(turns)
        turns_ref[j] = turns
        one = turn_cos_sin(turns * weight, SINE, COSINE)
        two = times(*one, *one)
        three = times(*two, *one)
        for power, (real, imag) in enumerate((one, two, three)):
            powers_ref[j, 2 * power] = real
            powers_ref[j, 2 * power + 1] = imag
        return 0

    lax.fori_loop(0, blocks, prepare, 0, unroll=2)
    total_ref[...] = jnp.zeros_like(total_ref)
    q_start = (iota((QROWS, 1), 0) * SLOTS - SUB // 2).astype(jnp.float32)
    r_start = (iota((QROWS, 1), 0) - SUB // 2).astype(jnp.float32)
    for copy in copies[2:]:
        copy.wait()
    for b in range(base_count):

        def one_block(j):
            sample = vis_ref[b, j].astype(jnp.float32)
            sample = jnp.where(j < used_ref[b], sample, 0.0)

            def fan(real, imag, line):
                reals, imags = [real], [imag]
                for power in range(SLOTS - 1):
                    power_real = powers_ref[j, 2 * power, line : line + 1, :]
                    power_imag = powers_ref[j, 2 * power + 1, line : line + 1, :]
                    next_real, next_imag = times(real, imag, power_real, power_imag)
                    reals.append(next_real)
                    imags.append(next_imag)
                return jnp.concatenate(reals + imags, axis=0).astype(jnp.bfloat16)

            base = turn_cos_sin(turns_ref[j, 2 * b : 2 * b + 1, :] * q_start, SINE, COSINE)
            left = fan(*times(*base, sample[0:1], sample[1:2]), 2 * b)
            right = fan(*turn_cos_sin(turns_ref[j, 2 * b + 1 : 2 * b + 2, :] * r_start, SINE, COSINE), 2 * b + 1)
            return lax.dot_general(left, right, (((1,), (1,)), ((), ())), preferred_element_type=jnp.float32)

        def two_blocks(half, sums):
            return sums + one_block(2 * half) + one_block(2 * half + 1)

        sums = lax.fori_loop(0, (used_ref[b] + 1) // 2, two_blocks, jnp.zeros((2 * SUB, 2 * SUB), jnp.float32))
        real = sums[:SUB, :SUB] - sums[SUB:, SUB:]
        imag = sums[:SUB, SUB:] + sums[SUB:, :SUB]
        image_ref[0:SUB, 0:SUB] = real * samples**-0.5
        image_ref[SUB : 2 * SUB, 0:SUB] = imag * samples**-0.5
        stations = iota((ROWS - 2 * SUB, LANES), 0)
        stations = jnp.where(stations == 0, pair_ref[0, b], jnp.where(stations == 1, pair_ref[1, b], 0))
        image_ref[2 * SUB :, :] = stations.astype(jnp.float32)
        image = jnp.where(iota((ROWS, LANES), 1) < SUB, image_ref[...], 0.0)
        row = row_ref[b]
        owner = row // base_count
        slot = row % base_count
        place = lax.rem(owner - me + axis_size, axis_size)
        total_ref[place, slot // SLOTS] += pltpu.roll(image, (slot % SLOTS) * SUB, 1)
    if len(send_refs) > 1:
        for place, send_ref in enumerate(send_refs):
            send_ref[...] = total_ref[place].astype(jnp.bfloat16)
    else:
        send_refs[0][...] = total_ref[...].astype(jnp.bfloat16)


def split_rows(value, rows_ref, first):
    for a in range(value.shape[1] // LANES):
        rows_ref[first + 2 * a : first + 2 * a + 2, :] = value[:, a * LANES : (a + 1) * LANES]


def swap(parts, lane):
    swapped = []
    for s in range(SLOTS):
        value = parts[s]
        for i in range(SLOTS):
            if i != s:
                value = jnp.where(lane // SUB == i, pltpu.roll(parts[i], ((i - s) % SLOTS) * SUB, 1), value)
        swapped.append(value)
    return swapped


def finish_kernel(payload_count, offset_hbm, table_hbm, *rest):
    payload_refs = rest[:payload_count]
    screens_refs = rest[payload_count:-6]
    out_ref, offset_ref, table_ref, rows_ref, screen_ref, sems = rest[-6:]
    copies = [
        pltpu.make_async_copy(offset_hbm, offset_ref, sems.at[0]),
        pltpu.make_async_copy(table_hbm, table_ref, sems.at[1]),
    ]
    for copy in copies:
        copy.start()
    base_count = out_ref.shape[1]
    groups = -(-base_count // SLOTS)
    me = lax.axis_index("sub")
    owners = lax.axis_size("sub")
    lane = iota((QROWS, LANES), 1)
    q = iota((QROWS, LANES), 0) * SLOTS + lane // SUB - SUB // 2
    r = lane % SUB - SUB // 2
    line = lambda h: 1.0 - (2.0 * h.astype(jnp.float32) / (SUB + 2)) ** 2
    taper = line(q) * line(r)

    def screen(station):
        if len(screens_refs) == 1:
            return screens_refs[0][0, station]
        here = screens_refs[0].shape[1]
        sent_from = station // here
        away = me ^ sent_from
        parts = [ref[0, station - sent_from * here] if len(ref.shape) == 4 else ref[station - sent_from * here] for ref in screens_refs]
        value = parts[0]
        for shift in range(1, owners):
            value = jnp.where(away == shift, parts[shift], value)
        return value

    for g in range(groups):
        parts = []
        for ref in payload_refs:
            parts += [ref[g]] if len(ref.shape) == 3 else [ref[p, g] for p in range(ref.shape[0])]
        whole = parts[0].astype(jnp.float32)
        for part in parts[1:]:
            whole = whole + part.astype(jnp.float32)
        rows_ref[...] = whole
        names = rows_ref[2 * SUB : 2 * SUB + 8, :].astype(jnp.int32)
        gains = []
        for s in range(SLOTS):
            pair = []
            for e in range(2):
                n = 2 * s + e
                split_rows(screen(names[e, s * SUB]).astype(jnp.float32), screen_ref.at[n], 0)
                pair.append((screen_ref[n, pl.ds(0, QROWS, stride=2), :], screen_ref[n, pl.ds(1, QROWS, stride=2), :]))
            (p_real, p_imag), (s_real, s_imag) = pair
            gains.append(times(p_real, -p_imag, s_real, s_imag))
        real = swap([rows_ref[i * QROWS : (i + 1) * QROWS, :] for i in range(SLOTS)], lane)
        imag = swap([rows_ref[SUB + i * QROWS : SUB + (i + 1) * QROWS, :] for i in range(SLOTS)], lane)
        if g == 0:
            for copy in copies:
                copy.wait()
        weighted = []
        for s in range(SLOTS):
            slot = g * SLOTS + s
            turn = lax.rem(offset_ref[0, slot] * q + offset_ref[1, slot] * r, SUB)
            cosine, sine = turn_cos_sin(turn.astype(jnp.float32) * (1.0 / SUB))
            centred = times(real[s], imag[s], cosine * taper, -sine * taper)
            weighted.append(times(*centred, *gains[s]))
        planes = swap([pair[0] for pair in weighted], lane) + swap([pair[1] for pair in weighted], lane)
        planes = jnp.concatenate(planes, axis=0)
        half = jnp.dot(planes, table_ref[:LANES], precision=HIGHEST, preferred_element_type=jnp.float32)
        half_real = half[:SUB, :LANES] + half[SUB:, LANES:]
        half_imag = half[SUB:, :LANES] - half[:SUB, LANES:]
        half = jnp.concatenate([half_real, half_imag], axis=0)
        full = jnp.dot(table_ref[LANES:, : 2 * SUB], half, precision=HIGHEST, preferred_element_type=jnp.float32)
        for c in range(2):
            flat = swap([full[c * SUB + i * QROWS : c * SUB + (i + 1) * QROWS] for i in range(SLOTS)], lane)
            for s in range(SLOTS):
                for a in range(QROWS):
                    out_ref[0, g * SLOTS + s, c : c + 1, a * LANES : (a + 1) * LANES] = flat[s][a : a + 1]


def tables():
    h = [n - SUB // 2 for n in range(SUB)]
    order = [(n % QROWS) * SLOTS + n // QROWS - SUB // 2 for n in range(SUB)]
    turn = lambda f, x, y: f(2.0 * math.pi * ((x * y) % SUB) / SUB)
    r_table = [
        [turn(f, h[m % SUB], h[n % SUB]) if m // SUB == n // SUB else 0.0 for f in (math.cos, math.sin) for n in range(LANES)]
        for m in range(LANES)
    ]
    cos = [[turn(math.cos, x, y) / SUB for y in order] for x in order]
    sin = [[turn(math.sin, x, y) / SUB for y in order] for x in order]
    q_table = [c + s for c, s in zip(cos, sin)] + [[-v for v in s] + c for c, s in zip(cos, sin)]
    return jnp.array(r_table + [row + [0.0] * (2 * LANES - 2 * SUB) for row in q_table], jnp.float32)


def local(
    visibilities, tracks, freq_ratio, blocks_used, subgrid_row, station_pair, subgrid_offsets, aterm_screens
):
    owners = lax.axis_size("sub")
    base_count, blocks, _, samples = visibilities.shape[1:]
    groups = -(-base_count // SLOTS)
    here, _, pixels = aterm_screens.shape[1:]
    vmem = pl.BlockSpec(memory_space=pltpu.VMEM)
    hbm = pl.BlockSpec(memory_space=pltpu.HBM)
    keep = lambda x: pltpu.with_memory_space_constraint(x, pltpu.HBM)
    shift_by = lambda x, shift: lax.ppermute(x, "sub", [(n, (n + shift) % owners) for n in range(owners)])
    direct = owners == 4
    if direct:
        flip = lambda x, bits: lax.ppermute(x, "sub", [(n, n ^ bits) for n in range(owners)])
        screens = [aterm_screens, flip(aterm_screens, 1), flip(aterm_screens, 2)]
        sends = [jax.ShapeDtypeStruct((groups, ROWS, LANES), jnp.bfloat16)] * owners
    else:
        sends = [jax.ShapeDtypeStruct((owners, groups, ROWS, LANES), jnp.bfloat16)]
    sent = pl.pallas_call(
        functools.partial(image_kernel, owners),
        out_shape=sends,
        in_specs=[hbm] * 6,
        out_specs=[vmem] * len(sends),
        scratch_shapes=[
            pltpu.SMEM((base_count,), jnp.int32),
            pltpu.SMEM((base_count,), jnp.int32),
            pltpu.SMEM((2, base_count), jnp.int32),
            pltpu.VMEM(visibilities.shape[1:], jnp.bfloat16),
            pltpu.VMEM(tracks.shape, jnp.float32),
            pltpu.VMEM(freq_ratio.shape, jnp.float32),
            pltpu.VMEM((2 * base_count, tracks.shape[-1]), jnp.float32),
            pltpu.VMEM((blocks, 2 * base_count, samples), jnp.float32),
            pltpu.VMEM((blocks, 2 * (SLOTS - 1), 2 * base_count, samples), jnp.float32),
            pltpu.VMEM((owners, groups, ROWS, LANES), jnp.float32),
            pltpu.SemaphoreType.DMA((6,)),
            pltpu.VMEM((8, LANES), jnp.float32),
            pltpu.VMEM((ROWS, LANES), jnp.float32),
        ],
        compiler_params=pltpu.CompilerParams(vmem_limit_bytes=48 * 1024 * 1024),
        name="images",
    )(*map(keep, (blocks_used, subgrid_row, station_pair.T, visibilities, tracks, freq_ratio)))
    if direct:
        sent, screens[2] = lax.optimization_barrier((list(sent), screens[2]))
        screens.append(flip(screens[2], 1))
        payloads = [sent[0]] + [shift_by(sent[shift], shift) for shift in range(1, owners)]
    else:
        by_owner = jnp.roll(sent[0], lax.axis_index("sub"), axis=0)
        payloads = [lax.all_to_all(by_owner, "sub", 0, 0, tiled=True)]
        screens = [lax.all_gather(aterm_screens, "sub", axis=1, tiled=True)]
    return pl.pallas_call(
        functools.partial(finish_kernel, len(payloads)),
        out_shape=jax.ShapeDtypeStruct((1, base_count, 2, pixels), jnp.float32),
        in_specs=[hbm] * 2 + [vmem] * (len(payloads) + len(screens)),
        out_specs=vmem,
        scratch_shapes=[
            pltpu.SMEM((2, base_count), jnp.int32),
            pltpu.VMEM((LANES + 2 * SUB, 2 * LANES), jnp.float32),
            pltpu.VMEM((ROWS, LANES), jnp.float32),
            pltpu.VMEM((2 * SLOTS, 2 * QROWS, LANES), jnp.float32),
            pltpu.SemaphoreType.DMA((2,)),
        ],
        compiler_params=pltpu.CompilerParams(vmem_limit_bytes=48 * 1024 * 1024),
        name="finish",
    )(keep(subgrid_offsets.T), keep(tables()), *payloads, *screens)


def solution(mesh):
    in_specs = (
        P("chan", ("grp", "sub"), None, None, None),
        P(("grp", "sub"), None, None),
        P(("grp", "chan"), None),
        P(("grp", "sub")),
        P(("grp", "sub")),
        P(("grp", "sub"), None),
        P(("grp", "sub"), None),
        P("chan", ("grp", "sub"), None, None),
    )
    out_specs = P("chan", ("grp", "sub"), None, None)
    return jax.shard_map(local, mesh=mesh, in_specs=in_specs, out_specs=out_specs, check_vma=False)
```

time: 37.8 us -> 21.5 us (0.57); the launches traced: 38.3 us -> 21.4 us
  blocking collectives: 15.9 us -> 0 us
  starting transfers between devices: 7.01 us -> 11.6 us
  Pallas kernels: 12.8 us -> 8.25 us
  local copies, waits for them, and re-layouts: 2.5 us -> 0.01 us
  waiting for transfers between devices: 0.01 us -> 1.49 us
    all_gather x1 -> x0, blocking collectives: 15.9 us -> none  [local(): screens = lax.all_gather(aterm_screens, 'sub', axis=1, tiled=True)]
    ppermute x3 -> x6, starting transfers between devices: 7.01 us -> 11.6 us  [the longest x3 5.92 us: local(): lax.ppermute(x, 'sub', [(n, (n + shift) % owners) for n in range(owners)])]
    pallas_call x1, Pallas kernels: 9.42 us -> 5.95 us  [local(): pl.pallas_call(functools.partial(image_kernel, owners), out_shape=sends,...]
    unnamed x16 -> x2, local copies, waits for them, and re-layouts: 2.5 us -> 0.01 us
    ppermute x3 -> x6, waiting for transfers between devices: 0.01 us -> 1.49 us  [the longest x3 1.48 us: local(): lax.ppermute(x, 'sub', [(n, (n + shift) % owners) for n in range(owners)])]
    pallas_call x2 -> x1, Pallas kernels: 3.38 us -> 2.3 us  [local(): pl.pallas_call(functools.partial(finish_kernel, len(payloads)), out_shape...]
  transfers between devices with their start and end apart: 3 -> 6, of which waited for: 0 -> 2; matrix products, arithmetic and copies ran while one was open for 0% -> 0% of each run, Pallas kernels for 0% -> 28%
where the time goes in v2:
time: 21.5 us; the launch traced here: 21.4 us
  starting transfers between devices  11.6 us (54%)
  Pallas kernels  8.25 us (38%)
  waiting for transfers between devices  1.49 us (7%)
    pallas_call x1, Pallas kernels, local(): pl.pallas_call(functools.partial(image_kernel, owners), out_shape=sends,...  5.95 us
    ppermute x3, starting transfers between devices, local(): lax.ppermute(x, 'sub', [(n, (n + shift) % owners) for n in range(owners)])  5.92 us
    ppermute x3, starting transfers between devices, local(): lax.ppermute(x, 'sub', [(n, n ^ bits) for n in range(owners)])  5.68 us
    pallas_call x1, Pallas kernels, local(): pl.pallas_call(functools.partial(finish_kernel, len(payloads)), out_shape...  2.3 us
    ppermute x3, waiting for transfers between devices, local(): lax.ppermute(x, 'sub', [(n, (n + shift) % owners) for n in range(owners)])  1.48 us
  transfers between devices with their start and end apart: 6, of which 2 were waited for; matrix products, arithmetic and copies ran while one was open for 0% of the time, Pallas kernels for 28%

profile of v2, /device:TPU:0, one launch (start us, length us, event | category | flops | bytes accessed | tf_op | source)
XLA Modules:
  0.0 21.4 jit_solution(6142458319748556140)
XLA Ops:
  0.0 0.0 copy-start
  0.0 4.0 %collective-permute-start = (bf16[1,32,2,1024]{3,2,1,0:T(2,128)(2,1)}, bf16[1,32,2,1024]{3,2,1,0:T(2,128)(2,1)S(1)}, u32[]{:S(2)}, u32[]{:S(2)}) collective-permute-start(bf16[1,32,2,1024]{3,2,1,0:T(2,128)(2,1)} %rest_4_.1), channel_id=1, source_target_pairs={{0,8},{4,12},{8,0},{12,4},{1,9},{5,13},{9,1},{13,5},{2,10},{6,14},... | collective-permute-start | bytes 393224 | tf_op jit(solution)/shard_map/ppermute | solution.py:262
  4.0 1.6 %collective-permute-start.4 = (bf16[1,32,2,1024]{3,2,1,0:T(2,128)(2,1)}, bf16[1,32,2,1024]{3,2,1,0:T(2,128)(2,1)S(1)}, u32[]{:S(2)}, u32[]{:S(2)}) collective-permute-start(bf16[1,32,2,1024]{3,2,1,0:T(2,128)(2,1)} %rest_4_.1), channel_id=1, source_target_pairs={{0,4},{4,0},{8,12},{12,8},{1,5},{5,1},{9,13},{13,9},{2,6},{6,2},{1... | collective-permute-start | bytes 393224 | tf_op jit(solution)/shard_map/ppermute | solution.py:262
  5.6 6.0 %images.1 = (bf16[1,80,128]{2,1,0:T(8,128)(2,1)S(1)}, bf16[1,80,128]{2,1,0:T(8,128)(2,1)S(1)}, bf16[1,80,128]{2,1,0:T(8,128)(2,1)S(1)}, bf16[1,80,128]{2,1,0:T(8,128)(2,1)S(1)}) custom-call(s32[4]{0:T(128)} %used_hbm.1, s32[4]{0:T(128)} %row_hbm.1, s32[2,4]{1,0:T(2,128)} %bitcast.2, bf16[1,4,8,2,1024]{4,3,2,1,0:T(2,128)(2,1)} %vis_hbm.1, ...), custom_call_target="tpu_custom_call" | custom-call | tf_op jit(solution)/shard_map/images/pallas_call | solution.py:267
  11.6 0.0 collective-permute-done.rest_6_
  11.6 0.1 collective-permute-start.5
  11.7 2.0 %collective-permute-start.1 = (bf16[1,80,128]{2,1,0:T(8,128)(2,1)S(1)}, bf16[1,80,128]{2,1,0:T(8,128)(2,1)S(1)}, u32[]{:S(2)}, u32[]{:S(2)}) collective-permute-start(bf16[1,80,128]{2,1,0:T(8,128)(2,1)S(1)} %get-tuple-element.19), channel_id=1, source_target_pairs={{0,4},{4,8},{8,12},{12,0},{1,5},{5,9},{9,13},{13,1},{2,6},{6,10},{... | collective-permute-start | bytes 61448 | tf_op jit(solution)/shard_map/ppermute | solution.py:259
  13.7 1.0 %collective-permute-start.2 = (bf16[1,80,128]{2,1,0:T(8,128)(2,1)S(1)}, bf16[1,80,128]{2,1,0:T(8,128)(2,1)S(1)}, u32[]{:S(2)}, u32[]{:S(2)}) collective-permute-start(bf16[1,80,128]{2,1,0:T(8,128)(2,1)S(1)} %get-tuple-element.20), channel_id=1, source_target_pairs={{0,8},{4,12},{8,0},{12,4},{1,9},{5,13},{9,1},{13,5},{2,10},{6,14},... | collective-permute-start | bytes 61448 | tf_op jit(solution)/shard_map/ppermute | solution.py:259
  14.7 2.9 %collective-permute-start.3 = (bf16[1,80,128]{2,1,0:T(8,128)(2,1)S(1)}, bf16[1,80,128]{2,1,0:T(8,128)(2,1)S(1)}, u32[]{:S(2)}, u32[]{:S(2)}) collective-permute-start(bf16[1,80,128]{2,1,0:T(8,128)(2,1)S(1)} %get-tuple-element.21), channel_id=1, source_target_pairs={{0,12},{4,0},{8,4},{12,8},{1,13},{5,1},{9,5},{13,9},{2,14},{6,2},{... | collective-permute-start | bytes 61448 | tf_op jit(solution)/shard_map/ppermute | solution.py:259
  17.6 0.0 collective-permute-done.4.rest_5_
  17.6 1.1 %collective-permute-done.1.rest_1_ = bf16[1,80,128]{2,1,0:T(8,128)(2,1)S(1)} collective-permute-done((bf16[1,80,128]{2,1,0:T(8,128)(2,1)S(1)}, bf16[1,80,128]{2,1,0:T(8,128)(2,1)S(1)}, u32[]{:S(2)}, u32[]{:S(2)}) %collective-permute-start.1) | collective-permute-done | bytes 20512 | tf_op jit(solution)/shard_map/ppermute | solution.py:259
  18.7 0.0 collective-permute-done.2.rest_2_
  18.7 0.4 %collective-permute-done.3.rest_3_ = bf16[1,80,128]{2,1,0:T(8,128)(2,1)S(1)} collective-permute-done((bf16[1,80,128]{2,1,0:T(8,128)(2,1)S(1)}, bf16[1,80,128]{2,1,0:T(8,128)(2,1)S(1)}, u32[]{:S(2)}, u32[]{:S(2)}) %collective-permute-start.3) | collective-permute-done | bytes 20512 | tf_op jit(solution)/shard_map/ppermute | solution.py:259
  19.1 0.0 collective-permute-done.5.rest_7_
  19.1 0.0 copy-done
  19.1 2.3 %finish.1 = f32[1,4,2,1024]{3,2,1,0:T(2,128)} custom-call(s32[2,4]{1,0:T(2,128)} %bitcast.3, f32[192,256]{1,0:T(8,128)} %constant.2.clone.table_hbm, bf16[1,80,128]{2,1,0:T(8,128)(2,1)S(1)} %get-tuple-element.18.rest_0_, bf16[1,80,128]{2,1,0:T(8,128)(2,1)S(1)} %collective-permute-done.1.rest_1_, bf16[1,80,128]{2,1,0:T(8,128)(2,1)S(1)} %collective-permute-done.2.rest_2_, ...), custom_call_target="tpu_custom_call" | custom-call | tf_op jit(solution)/shard_map/finish/pallas_call | solution.py:298
Async XLA Ops:
  0.0 19.1 %copy-start = (bf16[1,32,2,1024]{3,2,1,0:T(2,128)(2,1)S(1)}, bf16[1,32,2,1024]{3,2,1,0:T(2,128)(2,1)}, u32[]{:S(2)}) copy-start(bf16[1,32,2,1024]{3,2,1,0:T(2,128)(2,1)} %rest_4_.1) | copy-start | bytes 393220
  0.0 11.6 %collective-permute-start = (bf16[1,32,2,1024]{3,2,1,0:T(2,128)(2,1)}, bf16[1,32,2,1024]{3,2,1,0:T(2,128)(2,1)S(1)}, u32[]{:S(2)}, u32[]{:S(2)}) collective-permute-start(bf16[1,32,2,1024]{3,2,1,0:T(2,128)(2,1)} %rest_4_.1), channel_id=1, source_target_pairs={{0,8},{4,12},{8,0},{12,4},{1,9},{5,13},{9,1},{13,5},{2,10},{6,14},... | collective-permute-start | bytes 393224 | tf_op jit(solution)/shard_map/ppermute | solution.py:262
  4.0 13.5 %collective-permute-start.4 = (bf16[1,32,2,1024]{3,2,1,0:T(2,128)(2,1)}, bf16[1,32,2,1024]{3,2,1,0:T(2,128)(2,1)S(1)}, u32[]{:S(2)}, u32[]{:S(2)}) collective-permute-start(bf16[1,32,2,1024]{3,2,1,0:T(2,128)(2,1)} %rest_4_.1), channel_id=1, source_target_pairs={{0,4},{4,0},{8,12},{12,8},{1,5},{5,1},{9,13},{13,9},{2,6},{6,2},{1... | collective-permute-start | bytes 393224 | tf_op jit(solution)/shard_map/ppermute | solution.py:262
  11.6 7.5 %collective-permute-start.5 = (bf16[1,32,2,1024]{3,2,1,0:T(2,128)(2,1)S(1)}, bf16[1,32,2,1024]{3,2,1,0:T(2,128)(2,1)S(1)}, u32[]{:S(2)}, u32[]{:S(2)}) collective-permute-start(bf16[1,32,2,1024]{3,2,1,0:T(2,128)(2,1)S(1)} %collective-permute-done.rest_6_), channel_id=1, source_target_pairs={{0,4},{4,0},{8,12},{12,8},{1,5},{5,1},{9,13},{13,9},{2,6},{6,2},{1... | collective-permute-start | bytes 393224 | tf_op jit(solution)/shard_map/ppermute | solution.py:262
  11.7 7.0 %collective-permute-start.1 = (bf16[1,80,128]{2,1,0:T(8,128)(2,1)S(1)}, bf16[1,80,128]{2,1,0:T(8,128)(2,1)S(1)}, u32[]{:S(2)}, u32[]{:S(2)}) collective-permute-start(bf16[1,80,128]{2,1,0:T(8,128)(2,1)S(1)} %get-tuple-element.19), channel_id=1, source_target_pairs={{0,4},{4,8},{8,12},{12,0},{1,5},{5,9},{9,13},{13,1},{2,6},{6,10},{... | collective-permute-start | bytes 61448 | tf_op jit(solution)/shard_map/ppermute | solution.py:259
  13.7 5.0 %collective-permute-start.2 = (bf16[1,80,128]{2,1,0:T(8,128)(2,1)S(1)}, bf16[1,80,128]{2,1,0:T(8,128)(2,1)S(1)}, u32[]{:S(2)}, u32[]{:S(2)}) collective-permute-start(bf16[1,80,128]{2,1,0:T(8,128)(2,1)S(1)} %get-tuple-element.20), channel_id=1, source_target_pairs={{0,8},{4,12},{8,0},{12,4},{1,9},{5,13},{9,1},{13,5},{2,10},{6,14},... | collective-permute-start | bytes 61448 | tf_op jit(solution)/shard_map/ppermute | solution.py:259
  14.7 4.4 %collective-permute-start.3 = (bf16[1,80,128]{2,1,0:T(8,128)(2,1)S(1)}, bf16[1,80,128]{2,1,0:T(8,128)(2,1)S(1)}, u32[]{:S(2)}, u32[]{:S(2)}) collective-permute-start(bf16[1,80,128]{2,1,0:T(8,128)(2,1)S(1)} %get-tuple-element.21), channel_id=1, source_target_pairs={{0,12},{4,0},{8,4},{12,8},{1,13},{5,1},{9,5},{13,9},{2,14},{6,2},{... | collective-permute-start | bytes 61448 | tf_op jit(solution)/shard_map/ppermute | solution.py:259

commit v3 on v2

--- a/solution.py
+++ b/solution.py
@@ -13,6 +13,7 @@
 SLOTS = LANES // SUB
 QROWS = SUB // SLOTS
 ROWS = 2 * SUB + 16
+STEP = 8
 HIGHEST = lax.Precision.HIGHEST
 SINE = (3.14159027, -5.16740673, 2.54401052, -0.55946246)
 COSINE = (0.99999325, -4.93393467, 4.0412481, -1.22203176)
@@ -46,9 +47,9 @@
 def image_kernel(
     axis_size, used_hbm, row_hbm, pair_hbm, vis_hbm, tracks_hbm, freq_hbm, *rest
 ):
-    send_refs, scratch = rest[:-13], rest[-13:]
+    send_refs, scratch = rest[:-15], rest[-15:]
     (used_ref, row_ref, pair_ref, vis_ref, tracks_ref, freq_ref, lines_ref, turns_ref, powers_ref, total_ref,
-     sems, wide_ref, image_ref) = scratch
+     sems, wide_ref, image_ref, sums_ref, block_ref) = scratch
     base_count, blocks, _, samples = vis_ref.shape
     channels = freq_ref.shape[1]
     steps = samples // channels
@@ -91,35 +92,51 @@
 
     lax.fori_loop(0, blocks, prepare, 0, unroll=2)
     total_ref[...] = jnp.zeros_like(total_ref)
+    sums_ref[...] = jnp.zeros_like(sums_ref)
     q_start = (iota((QROWS, 1), 0) * SLOTS - SUB // 2).astype(jnp.float32)
     r_start = (iota((QROWS, 1), 0) - SUB // 2).astype(jnp.float32)
     for copy in copies[2:]:
         copy.wait()
+
+    count = jnp.int32(0)
     for b in range(base_count):
 
-        def one_block(j):
+        def note(j, _):
+            block_ref[count + j] = b * blocks + j
+            return 0
+
+        lax.fori_loop(0, used_ref[b], note, 0)
+        count = count + used_ref[b]
+    for n in range(STEP - 1):
+        block_ref[count + n] = 0
+
+    def some_blocks(step, _):
+        for n in range(STEP):
+            block = block_ref[step * STEP + n]
+            b, j = block // blocks, block % blocks
             sample = vis_ref[b, j].astype(jnp.float32)
-            sample = jnp.where(j < used_ref[b], sample, 0.0)
+            sample = jnp.where(step * STEP + n < count, sample, 0.0)
 
             def fan(real, imag, line):
                 reals, imags = [real], [imag]
                 for power in range(SLOTS - 1):
-                    power_real = powers_ref[j, 2 * power, line : line + 1, :]
-                    power_imag = powers_ref[j, 2 * power + 1, line : line + 1, :]
+                    power_real = powers_ref[j, 2 * power, pl.ds(line, 1), :]
+                    power_imag = powers_ref[j, 2 * power + 1, pl.ds(line, 1), :]
                     next_real, next_imag = times(real, imag, power_real, power_imag)
                     reals.append(next_real)
                     imags.append(next_imag)
                 return jnp.concatenate(reals + imags, axis=0).astype(jnp.bfloat16)
 
-            base = turn_cos_sin(turns_ref[j, 2 * b : 2 * b + 1, :] * q_start, SINE, COSINE)
+            turns = [turns_ref[j, pl.ds(2 * b + axis, 1), :] for axis in range(2)]
+            base = turn_cos_sin(turns[0] * q_start, SINE, COSINE)
             left = fan(*times(*base, sample[0:1], sample[1:2]), 2 * b)
-            right = fan(*turn_cos_sin(turns_ref[j, 2 * b + 1 : 2 * b + 2, :] * r_start, SINE, COSINE), 2 * b + 1)
-            return lax.dot_general(left, right, (((1,), (1,)), ((), ())), preferred_element_type=jnp.float32)
-
-        def two_blocks(half, sums):
-            return sums + one_block(2 * half) + one_block(2 * half + 1)
-
-        sums = lax.fori_loop(0, (used_ref[b] + 1) // 2, two_blocks, jnp.zeros((2 * SUB, 2 * SUB), jnp.float32))
+            right = fan(*turn_cos_sin(turns[1] * r_start, SINE, COSINE), 2 * b + 1)
+            sums_ref[b] += lax.dot_general(left, right, (((1,), (1,)), ((), ())), preferred_element_type=jnp.float32)
+        return 0
+
+    lax.fori_loop(0, (count + STEP - 1) // STEP, some_blocks, 0)
+    for b in range(base_count):
+        sums = sums_ref[b]
         real = sums[:SUB, :SUB] - sums[SUB:, SUB:]
         imag = sums[:SUB, SUB:] + sums[SUB:, :SUB]
         image_ref[0:SUB, 0:SUB] = real * samples**-0.5
@@ -156,39 +173,18 @@
     return swapped
 
 
-def finish_kernel(payload_count, offset_hbm, table_hbm, *rest):
-    payload_refs = rest[:payload_count]
-    screens_refs = rest[payload_count:-6]
-    out_ref, offset_ref, table_ref, rows_ref, screen_ref, sems = rest[-6:]
-    copies = [
-        pltpu.make_async_copy(offset_hbm, offset_ref, sems.at[0]),
-        pltpu.make_async_copy(table_hbm, table_ref, sems.at[1]),
-    ]
-    for copy in copies:
-        copy.start()
-    base_count = out_ref.shape[1]
-    groups = -(-base_count // SLOTS)
-    me = lax.axis_index("sub")
-    owners = lax.axis_size("sub")
+def subgrid_kernel(offset_hbm, table_hbm, *rest):
+    payload_refs, (pixels_ref, station_ref, table_ref, offset_ref, rows_ref, sems) = rest[:-6], rest[-6:]
+    copy = pltpu.make_async_copy(offset_hbm, offset_ref, sems.at[0])
+    copy.start()
+    table_copy = pltpu.make_async_copy(table_hbm, table_ref, sems.at[1])
+    table_copy.start()
     lane = iota((QROWS, LANES), 1)
     q = iota((QROWS, LANES), 0) * SLOTS + lane // SUB - SUB // 2
     r = lane % SUB - SUB // 2
     line = lambda h: 1.0 - (2.0 * h.astype(jnp.float32) / (SUB + 2)) ** 2
     taper = line(q) * line(r)
-
-    def screen(station):
-        if len(screens_refs) == 1:
-            return screens_refs[0][0, station]
-        here = screens_refs[0].shape[1]
-        sent_from = station // here
-        away = me ^ sent_from
-        parts = [ref[0, station - sent_from * here] if len(ref.shape) == 4 else ref[station - sent_from * here] for ref in screens_refs]
-        value = parts[0]
-        for shift in range(1, owners):
-            value = jnp.where(away == shift, parts[shift], value)
-        return value
-
-    for g in range(groups):
+    for g in range(pixels_ref.shape[0] // SLOTS):
         parts = []
         for ref in payload_refs:
             parts += [ref[g]] if len(ref.shape) == 3 else [ref[p, g] for p in range(ref.shape[0])]
@@ -196,28 +192,47 @@
         for part in parts[1:]:
             whole = whole + part.astype(jnp.float32)
         rows_ref[...] = whole
-        names = rows_ref[2 * SUB : 2 * SUB + 8, :].astype(jnp.int32)
-        gains = []
+        station_ref[g] = rows_ref[2 * SUB : 2 * SUB + 8, :].astype(jnp.int32)
+        real = swap([rows_ref[i * QROWS : (i + 1) * QROWS, :] for i in range(SLOTS)], lane)
+        imag = swap([rows_ref[SUB + i * QROWS : SUB + (i + 1) * QROWS, :] for i in range(SLOTS)], lane)
+        if g == 0:
+            copy.wait()
         for s in range(SLOTS):
+            slot = g * SLOTS + s
+            turn = lax.rem(offset_ref[0, slot] * q + offset_ref[1, slot] * r, SUB)
+            cosine, sine = turn_cos_sin(turn.astype(jnp.float32) * (1.0 / SUB))
+            pixels_ref[slot, 0], pixels_ref[slot, 1] = times(real[s], imag[s], cosine * taper, -sine * taper)
+    table_copy.wait()
+
+
+def finish_kernel(table_ref, station_ref, pixels_ref, *rest):
+    screens_refs, (out_ref, screen_ref) = rest[:-2], rest[-2:]
+    me = lax.axis_index("sub")
+    lane = iota((QROWS, LANES), 1)
+
+    def screen(station):
+        if len(screens_refs) == 1:
+            return screens_refs[0][0, station]
+        here = screens_refs[0].shape[1]
+        away = me ^ (station // here)
+        value = screens_refs[0][0, station % here]
+        for flips in range(1, len(screens_refs)):
+            value = jnp.where(away == flips, screens_refs[flips][0, station % here], value)
+        return value
+
+    for g in range(pixels_ref.shape[0] // SLOTS):
+        weighted = []
+        names = station_ref[g]
+        for s in range(SLOTS):
+            slot = g * SLOTS + s
             pair = []
             for e in range(2):
                 n = 2 * s + e
                 split_rows(screen(names[e, s * SUB]).astype(jnp.float32), screen_ref.at[n], 0)
                 pair.append((screen_ref[n, pl.ds(0, QROWS, stride=2), :], screen_ref[n, pl.ds(1, QROWS, stride=2), :]))
             (p_real, p_imag), (s_real, s_imag) = pair
-            gains.append(times(p_real, -p_imag, s_real, s_imag))
-        real = swap([rows_ref[i * QROWS : (i + 1) * QROWS, :] for i in range(SLOTS)], lane)
-        imag = swap([rows_ref[SUB + i * QROWS : SUB + (i + 1) * QROWS, :] for i in range(SLOTS)], lane)
-        if g == 0:
-            for copy in copies:
-                copy.wait()
-        weighted = []
-        for s in range(SLOTS):
-            slot = g * SLOTS + s
-            turn = lax.rem(offset_ref[0, slot] * q + offset_ref[1, slot] * r, SUB)
-            cosine, sine = turn_cos_sin(turn.astype(jnp.float32) * (1.0 / SUB))
-            centred = times(real[s], imag[s], cosine * taper, -sine * taper)
-            weighted.append(times(*centred, *gains[s]))
+            gain = times(p_real, -p_imag, s_real, s_imag)
+            weighted.append(times(pixels_ref[slot, 0], pixels_ref[slot, 1], *gain))
         planes = swap([pair[0] for pair in weighted], lane) + swap([pair[1] for pair in weighted], lane)
         planes = jnp.concatenate(planes, axis=0)
         half = jnp.dot(planes, table_ref[:LANES], precision=HIGHEST, preferred_element_type=jnp.float32)
@@ -283,33 +298,50 @@
             pltpu.SemaphoreType.DMA((6,)),
             pltpu.VMEM((8, LANES), jnp.float32),
             pltpu.VMEM((ROWS, LANES), jnp.float32),
+            pltpu.VMEM((base_count, 2 * SUB, 2 * SUB), jnp.float32),
+            pltpu.SMEM((base_count * blocks + STEP - 1,), jnp.int32),
         ],
         compiler_params=pltpu.CompilerParams(vmem_limit_bytes=48 * 1024 * 1024),
         name="images",
     )(*map(keep, (blocks_used, subgrid_row, station_pair.T, visibilities, tracks, freq_ratio)))
     if direct:
-        sent, screens[2] = lax.optimization_barrier((list(sent), screens[2]))
+        payloads = [sent[0]] + [shift_by(sent[shift], shift) for shift in range(1, owners)]
+        payloads[0], screens[2] = lax.optimization_barrier((payloads[0], screens[2]))
         screens.append(flip(screens[2], 1))
-        payloads = [sent[0]] + [shift_by(sent[shift], shift) for shift in range(1, owners)]
+        payloads[0], screens[1] = lax.optimization_barrier((payloads[0], screens[1]))
     else:
         by_owner = jnp.roll(sent[0], lax.axis_index("sub"), axis=0)
         payloads = [lax.all_to_all(by_owner, "sub", 0, 0, tiled=True)]
         screens = [lax.all_gather(aterm_screens, "sub", axis=1, tiled=True)]
-    return pl.pallas_call(
-        functools.partial(finish_kernel, len(payloads)),
-        out_shape=jax.ShapeDtypeStruct((1, base_count, 2, pixels), jnp.float32),
-        in_specs=[hbm] * 2 + [vmem] * (len(payloads) + len(screens)),
-        out_specs=vmem,
+    subgrids, stations, table = pl.pallas_call(
+        subgrid_kernel,
+        out_shape=[
+            jax.ShapeDtypeStruct((base_count, 2, QROWS, LANES), jnp.float32),
+            jax.ShapeDtypeStruct((groups, 8, LANES), jnp.int32),
+            jax.ShapeDtypeStruct((LANES + 2 * SUB, 2 * LANES), jnp.float32),
+        ],
+        in_specs=[hbm] * 2 + [vmem] * len(payloads),
+        out_specs=[vmem] * 3,
         scratch_shapes=[
             pltpu.SMEM((2, base_count), jnp.int32),
-            pltpu.VMEM((LANES + 2 * SUB, 2 * LANES), jnp.float32),
             pltpu.VMEM((ROWS, LANES), jnp.float32),
-            pltpu.VMEM((2 * SLOTS, 2 * QROWS, LANES), jnp.float32),
             pltpu.SemaphoreType.DMA((2,)),
         ],
         compiler_params=pltpu.CompilerParams(vmem_limit_bytes=48 * 1024 * 1024),
+        cost_estimate=pl.CostEstimate(flops=30000000000, bytes_accessed=100000, transcendentals=0),
+        name="subgrids",
+    )(keep(subgrid_offsets.T), keep(tables()), *payloads)
+    return pl.pallas_call(
+        finish_kernel,
+        out_shape=jax.ShapeDtypeStruct((1, base_count, 2, pixels), jnp.float32),
+        in_specs=[vmem] * (3 + len(screens)),
+        out_specs=vmem,
+        scratch_shapes=[
+            pltpu.VMEM((2 * SLOTS, 2 * QROWS, LANES), jnp.float32),
+        ],
+        compiler_params=pltpu.CompilerParams(vmem_limit_bytes=48 * 1024 * 1024),
         name="finish",
-    )(keep(subgrid_offsets.T), keep(tables()), *payloads, *screens)
+    )(table, stations, subgrids, *screens)
 
 
 def solution(mesh):

time: 21.5 us -> 20.3 us (0.944)
  waiting for transfers between devices: 1.49 us -> 3.35 us
  Pallas kernels: 8.25 us -> 6.64 us
  starting transfers between devices: 11.6 us -> 10.1 us
    ppermute x3, starting transfers between devices: 5.92 us -> 3.88 us  [local(): lax.ppermute(x, 'sub', [(n, (n + shift) % owners) for n in range(owners)])]
    pallas_call x1, Pallas kernels: 5.95 us -> 4.31 us  [local(): pl.pallas_call(functools.partial(image_kernel, owners), out_shape=sends,...]
    ppermute x3, waiting for transfers between devices: 0.01 us -> 1.49 us  [local(): lax.ppermute(x, 'sub', [(n, n ^ bits) for n in range(owners)])]
    ppermute x3, starting transfers between devices: 5.68 us -> 6.24 us  [local(): lax.ppermute(x, 'sub', [(n, n ^ bits) for n in range(owners)])]
    ppermute x3, waiting for transfers between devices: 1.48 us -> 1.86 us  [local(): lax.ppermute(x, 'sub', [(n, (n + shift) % owners) for n in range(owners)])]
    pallas_call x1 -> x2, Pallas kernels: 2.3 us -> 2.33 us  [the longest x1 1.35 us: local(): pl.pallas_call(finish_kernel, out_shape=jax.ShapeDtypeStruct((1, base_cou...]
  transfers between devices with their start and end apart: 6 -> 6, of which waited for: 2 -> 3; matrix products, arithmetic and copies ran while one was open for 0% -> 0% of each run, Pallas kernels for 28% -> 26%
where the time goes in v3:
time: 20.3 us; the launch traced here: 20.1 us
  starting transfers between devices  10.1 us (50%)
  Pallas kernels  6.64 us (33%)
  waiting for transfers between devices  3.35 us (17%)
    ppermute x3, starting transfers between devices, local(): lax.ppermute(x, 'sub', [(n, n ^ bits) for n in range(owners)])  6.24 us
    pallas_call x1, Pallas kernels, local(): pl.pallas_call(functools.partial(image_kernel, owners), out_shape=sends,...  4.31 us
    ppermute x3, starting transfers between devices, local(): lax.ppermute(x, 'sub', [(n, (n + shift) % owners) for n in range(owners)])  3.88 us
    ppermute x3, waiting for transfers between devices, local(): lax.ppermute(x, 'sub', [(n, (n + shift) % owners) for n in range(owners)])  1.86 us
    ppermute x3, waiting for transfers between devices, local(): lax.ppermute(x, 'sub', [(n, n ^ bits) for n in range(owners)])  1.49 us
    pallas_call x1, Pallas kernels, local(): pl.pallas_call(finish_kernel, out_shape=jax.ShapeDtypeStruct((1, base_cou...  1.35 us
    pallas_call x1, Pallas kernels, local(): pl.pallas_call(subgrid_kernel, out_shape=[jax.ShapeDtypeStruct((base_coun...  0.98 us
  transfers between devices with their start and end apart: 6, of which 3 were waited for; matrix products, arithmetic and copies ran while one was open for 0% of the time, Pallas kernels for 26%

profile of v3, /device:TPU:0, one launch (start us, length us, event | category | flops | bytes accessed | tf_op | source)
XLA Modules:
  0.0 20.1 jit_solution(13502619992883645807)
XLA Ops:
  0.0 4.0 %collective-permute-start = (bf16[1,32,2,1024]{3,2,1,0:T(2,128)(2,1)}, bf16[1,32,2,1024]{3,2,1,0:T(2,128)(2,1)S(1)}, u32[]{:S(2)}, u32[]{:S(2)}) collective-permute-start(bf16[1,32,2,1024]{3,2,1,0:T(2,128)(2,1)} %rest_0_.1), channel_id=1, source_target_pairs={{0,8},{4,12},{8,0},{12,4},{1,9},{5,13},{9,1},{13,5},{2,10},{6,14},... | collective-permute-start | bytes 393224 | tf_op jit(solution)/shard_map/ppermute | solution.py:277
  4.0 1.6 %collective-permute-start.1 = (bf16[1,32,2,1024]{3,2,1,0:T(2,128)(2,1)}, bf16[1,32,2,1024]{3,2,1,0:T(2,128)(2,1)S(1)}, u32[]{:S(2)}, u32[]{:S(2)}) collective-permute-start(bf16[1,32,2,1024]{3,2,1,0:T(2,128)(2,1)} %rest_0_.1), channel_id=1, source_target_pairs={{0,4},{4,0},{8,12},{12,8},{1,5},{5,1},{9,13},{13,9},{2,6},{6,2},{1... | collective-permute-start | bytes 393224 | tf_op jit(solution)/shard_map/ppermute | solution.py:277
  5.6 4.3 %images.1 = (bf16[1,80,128]{2,1,0:T(8,128)(2,1)S(1)}, bf16[1,80,128]{2,1,0:T(8,128)(2,1)S(1)}, bf16[1,80,128]{2,1,0:T(8,128)(2,1)S(1)}, bf16[1,80,128]{2,1,0:T(8,128)(2,1)S(1)}) custom-call(s32[4]{0:T(128)} %used_hbm.1, s32[4]{0:T(128)} %row_hbm.1, s32[2,4]{1,0:T(2,128)} %bitcast.2, bf16[1,4,8,2,1024]{4,3,2,1,0:T(2,128)(2,1)} %vis_hbm.1, ...), custom_call_target="tpu_custom_call" | custom-call | tf_op jit(solution)/shard_map/images/pallas_call | solution.py:282
  9.9 0.5 %collective-permute-start.2 = (bf16[1,80,128]{2,1,0:T(8,128)(2,1)S(1)}, bf16[1,80,128]{2,1,0:T(8,128)(2,1)S(1)}, u32[]{:S(2)}, u32[]{:S(2)}) collective-permute-start(bf16[1,80,128]{2,1,0:T(8,128)(2,1)S(1)} %get-tuple-element.19), channel_id=1, source_target_pairs={{0,4},{4,8},{8,12},{12,0},{1,5},{5,9},{9,13},{13,1},{2,6},{6,10},{... | collective-permute-start | bytes 61448 | tf_op jit(solution)/shard_map/ppermute | solution.py:274
  10.4 0.0 collective-permute-start.3
  10.4 3.4 %collective-permute-start.4 = (bf16[1,80,128]{2,1,0:T(8,128)(2,1)S(1)}, bf16[1,80,128]{2,1,0:T(8,128)(2,1)S(1)}, u32[]{:S(2)}, u32[]{:S(2)}) collective-permute-start(bf16[1,80,128]{2,1,0:T(8,128)(2,1)S(1)} %get-tuple-element.21), channel_id=1, source_target_pairs={{0,12},{4,0},{8,4},{12,8},{1,13},{5,1},{9,5},{13,9},{2,14},{6,2},{... | collective-permute-start | bytes 61448 | tf_op jit(solution)/shard_map/ppermute | solution.py:274
  13.8 0.0 collective-permute-done.rest_2_
  13.8 0.0 collective-permute-done.1.rest_1_
  13.8 0.6 %collective-permute-start.5 = (bf16[1,32,2,1024]{3,2,1,0:T(2,128)(2,1)S(1)}, bf16[1,32,2,1024]{3,2,1,0:T(2,128)(2,1)S(1)}, u32[]{:S(2)}, u32[]{:S(2)}) collective-permute-start(bf16[1,32,2,1024]{3,2,1,0:T(2,128)(2,1)S(1)} %collective-permute-done.rest_2_), channel_id=1, source_target_pairs={{0,4},{4,0},{8,12},{12,8},{1,5},{5,1},{9,13},{13,9},{2,6},{6,2},{1... | collective-permute-start | bytes 393224 | tf_op jit(solution)/shard_map/ppermute | solution.py:277
  14.5 1.2 %collective-permute-done.2.rest_1_ = bf16[1,80,128]{2,1,0:T(8,128)(2,1)S(1)} collective-permute-done((bf16[1,80,128]{2,1,0:T(8,128)(2,1)S(1)}, bf16[1,80,128]{2,1,0:T(8,128)(2,1)S(1)}, u32[]{:S(2)}, u32[]{:S(2)}) %collective-permute-start.2) | collective-permute-done | bytes 20512 | tf_op jit(solution)/shard_map/ppermute | solution.py:274
  15.7 0.0 collective-permute-done.3.rest_2_
  15.7 0.6 %collective-permute-done.4.rest_3_ = bf16[1,80,128]{2,1,0:T(8,128)(2,1)S(1)} collective-permute-done((bf16[1,80,128]{2,1,0:T(8,128)(2,1)S(1)}, bf16[1,80,128]{2,1,0:T(8,128)(2,1)S(1)}, u32[]{:S(2)}, u32[]{:S(2)}) %collective-permute-start.4) | collective-permute-done | bytes 20512 | tf_op jit(solution)/shard_map/ppermute | solution.py:274
  16.3 0.0 copy-start
  16.3 1.0 %subgrids.1 = (f32[4,2,8,128]{3,2,1,0:T(8,128)S(1)}, s32[1,8,128]{2,1,0:T(8,128)S(1)}, f32[192,256]{1,0:T(8,128)S(1)}) custom-call(s32[2,4]{1,0:T(2,128)} %bitcast.3, f32[192,256]{1,0:T(8,128)} %constant.2.clone.table_hbm, bf16[1,80,128]{2,1,0:T(8,128)(2,1)S(1)} %get-tuple-element.18.rest_0_, bf16[1,80,128]{2,1,0:T(8,128)(2,1)S(1)} %collective-permute-done.2.rest_1_, ...), custom_call_target="tpu_custom_call" | custom-call | flops 30000001024 | bytes 100000 | tf_op jit(solution)/shard_map/subgrids/pallas_call | solution.py:316
  17.3 1.5 %collective-permute-done.5.rest_3_ = bf16[1,32,2,1024]{3,2,1,0:T(2,128)(2,1)S(1)} collective-permute-done((bf16[1,32,2,1024]{3,2,1,0:T(2,128)(2,1)S(1)}, bf16[1,32,2,1024]{3,2,1,0:T(2,128)(2,1)S(1)}, u32[]{:S(2)}, u32[]{:S(2)}) %collective-permute-start.5) | collective-permute-done | bytes 131104 | tf_op jit(solution)/shard_map/ppermute | solution.py:277
  18.8 0.0 copy-done
  18.8 1.3 %finish.1 = f32[1,4,2,1024]{3,2,1,0:T(2,128)} custom-call(f32[192,256]{1,0:T(8,128)S(1)} %get-tuple-element.22.table_ref, s32[1,8,128]{2,1,0:T(8,128)S(1)} %get-tuple-element.23.station_ref, f32[4,2,8,128]{3,2,1,0:T(8,128)S(1)} %get-tuple-element.24.pixels_ref, bf16[1,32,2,1024]{3,2,1,0:T(2,128)(2,1)S(1)} %copy-done, ...), custom_call_target="tpu_custom_call" | custom-call | tf_op jit(solution)/shard_map/finish/pallas_call | solution.py:334
Async XLA Ops:
  0.0 13.8 %collective-permute-start = (bf16[1,32,2,1024]{3,2,1,0:T(2,128)(2,1)}, bf16[1,32,2,1024]{3,2,1,0:T(2,128)(2,1)S(1)}, u32[]{:S(2)}, u32[]{:S(2)}) collective-permute-start(bf16[1,32,2,1024]{3,2,1,0:T(2,128)(2,1)} %rest_0_.1), channel_id=1, source_target_pairs={{0,8},{4,12},{8,0},{12,4},{1,9},{5,13},{9,1},{13,5},{2,10},{6,14},... | collective-permute-start | bytes 393224 | tf_op jit(solution)/shard_map/ppermute | solution.py:277
  4.0 9.8 %collective-permute-start.1 = (bf16[1,32,2,1024]{3,2,1,0:T(2,128)(2,1)}, bf16[1,32,2,1024]{3,2,1,0:T(2,128)(2,1)S(1)}, u32[]{:S(2)}, u32[]{:S(2)}) collective-permute-start(bf16[1,32,2,1024]{3,2,1,0:T(2,128)(2,1)} %rest_0_.1), channel_id=1, source_target_pairs={{0,4},{4,0},{8,12},{12,8},{1,5},{5,1},{9,13},{13,9},{2,6},{6,2},{1... | collective-permute-start | bytes 393224 | tf_op jit(solution)/shard_map/ppermute | solution.py:277
  9.9 5.7 %collective-permute-start.2 = (bf16[1,80,128]{2,1,0:T(8,128)(2,1)S(1)}, bf16[1,80,128]{2,1,0:T(8,128)(2,1)S(1)}, u32[]{:S(2)}, u32[]{:S(2)}) collective-permute-start(bf16[1,80,128]{2,1,0:T(8,128)(2,1)S(1)} %get-tuple-element.19), channel_id=1, source_target_pairs={{0,4},{4,8},{8,12},{12,0},{1,5},{5,9},{9,13},{13,1},{2,6},{6,10},{... | collective-permute-start | bytes 61448 | tf_op jit(solution)/shard_map/ppermute | solution.py:274
  10.4 5.3 %collective-permute-start.3 = (bf16[1,80,128]{2,1,0:T(8,128)(2,1)S(1)}, bf16[1,80,128]{2,1,0:T(8,128)(2,1)S(1)}, u32[]{:S(2)}, u32[]{:S(2)}) collective-permute-start(bf16[1,80,128]{2,1,0:T(8,128)(2,1)S(1)} %get-tuple-element.20), channel_id=1, source_target_pairs={{0,8},{4,12},{8,0},{12,4},{1,9},{5,13},{9,1},{13,5},{2,10},{6,14},... | collective-permute-start | bytes 61448 | tf_op jit(solution)/shard_map/ppermute | solution.py:274
  10.4 5.9 %collective-permute-start.4 = (bf16[1,80,128]{2,1,0:T(8,128)(2,1)S(1)}, bf16[1,80,128]{2,1,0:T(8,128)(2,1)S(1)}, u32[]{:S(2)}, u32[]{:S(2)}) collective-permute-start(bf16[1,80,128]{2,1,0:T(8,128)(2,1)S(1)} %get-tuple-element.21), channel_id=1, source_target_pairs={{0,12},{4,0},{8,4},{12,8},{1,13},{5,1},{9,5},{13,9},{2,14},{6,2},{... | collective-permute-start | bytes 61448 | tf_op jit(solution)/shard_map/ppermute | solution.py:274
  13.8 5.0 %collective-permute-start.5 = (bf16[1,32,2,1024]{3,2,1,0:T(2,128)(2,1)S(1)}, bf16[1,32,2,1024]{3,2,1,0:T(2,128)(2,1)S(1)}, u32[]{:S(2)}, u32[]{:S(2)}) collective-permute-start(bf16[1,32,2,1024]{3,2,1,0:T(2,128)(2,1)S(1)} %collective-permute-done.rest_2_), channel_id=1, source_target_pairs={{0,4},{4,0},{8,12},{12,8},{1,5},{5,1},{9,13},{13,9},{2,6},{6,2},{1... | collective-permute-start | bytes 393224 | tf_op jit(solution)/shard_map/ppermute | solution.py:277
  16.3 2.5 %copy-start = (bf16[1,32,2,1024]{3,2,1,0:T(2,128)(2,1)S(1)}, bf16[1,32,2,1024]{3,2,1,0:T(2,128)(2,1)}, u32[]{:S(2)}) copy-start(bf16[1,32,2,1024]{3,2,1,0:T(2,128)(2,1)} %rest_0_.1) | copy-start | bytes 393220

commit v4 on v3

--- a/solution.py
+++ b/solution.py
@@ -45,9 +45,9 @@
 
 
 def image_kernel(
-    axis_size, used_hbm, row_hbm, pair_hbm, vis_hbm, tracks_hbm, freq_hbm, *rest
+    axis_size, used_hbm, row_hbm, pair_hbm, vis_hbm, tracks_hbm, freq_hbm, table_hbm, *rest
 ):
-    send_refs, scratch = rest[:-15], rest[-15:]
+    send_refs, table_ref, scratch = rest[:-16], rest[-16], rest[-15:]
     (used_ref, row_ref, pair_ref, vis_ref, tracks_ref, freq_ref, lines_ref, turns_ref, powers_ref, total_ref,
      sems, wide_ref, image_ref, sums_ref, block_ref) = scratch
     base_count, blocks, _, samples = vis_ref.shape
@@ -59,7 +59,7 @@
     tiles = samples // LANES
     sources = (
         (tracks_hbm, tracks_ref), (freq_hbm, freq_ref), (used_hbm, used_ref), (vis_hbm.at[0], vis_ref),
-        (row_hbm, row_ref), (pair_hbm, pair_ref),
+        (row_hbm, row_ref), (pair_hbm, pair_ref), (table_hbm, table_ref),
     )
     copies = [pltpu.make_async_copy(one, two, sems.at[n]) for n, (one, two) in enumerate(sources)]
     for copy in copies:
@@ -84,18 +84,17 @@
         turns_ref[j] = turns
         one = turn_cos_sin(turns * weight, SINE, COSINE)
         two = times(*one, *one)
-        three = times(*two, *one)
-        for power, (real, imag) in enumerate((one, two, three)):
+        for power, (real, imag) in enumerate((one, two)):
             powers_ref[j, 2 * power] = real
             powers_ref[j, 2 * power + 1] = imag
         return 0
 
-    lax.fori_loop(0, blocks, prepare, 0, unroll=2)
+    lax.fori_loop(0, blocks, prepare, 0, unroll=blocks if lines <= 8 else 1)
     total_ref[...] = jnp.zeros_like(total_ref)
     sums_ref[...] = jnp.zeros_like(sums_ref)
     q_start = (iota((QROWS, 1), 0) * SLOTS - SUB // 2).astype(jnp.float32)
-    r_start = (iota((QROWS, 1), 0) - SUB // 2).astype(jnp.float32)
-    for copy in copies[2:]:
+    r_start = iota((QROWS, 1), 0).astype(jnp.float32) + 0.5
+    for copy in copies[2:-1]:
         copy.wait()
 
     count = jnp.int32(0)
@@ -117,30 +116,27 @@
             sample = vis_ref[b, j].astype(jnp.float32)
             sample = jnp.where(step * STEP + n < count, sample, 0.0)
 
-            def fan(real, imag, line):
-                reals, imags = [real], [imag]
-                for power in range(SLOTS - 1):
-                    power_real = powers_ref[j, 2 * power, pl.ds(line, 1), :]
-                    power_imag = powers_ref[j, 2 * power + 1, pl.ds(line, 1), :]
-                    next_real, next_imag = times(real, imag, power_real, power_imag)
-                    reals.append(next_real)
-                    imags.append(next_imag)
-                return jnp.concatenate(reals + imags, axis=0).astype(jnp.bfloat16)
+            def power(n, line):
+                return powers_ref[j, 2 * n, pl.ds(line, 1), :], powers_ref[j, 2 * n + 1, pl.ds(line, 1), :]
 
             turns = [turns_ref[j, pl.ds(2 * b + axis, 1), :] for axis in range(2)]
-            base = turn_cos_sin(turns[0] * q_start, SINE, COSINE)
-            left = fan(*times(*base, sample[0:1], sample[1:2]), 2 * b)
-            right = fan(*turn_cos_sin(turns[1] * r_start, SINE, COSINE), 2 * b + 1)
+            one = power(0, 2 * b)
+            first = turn_cos_sin(turns[0] * q_start - turns[1] * 0.5, SINE, COSINE)
+            first = times(*first, sample[0:1], sample[1:2])
+            third = times(*first, *power(1, 2 * b))
+            left = [first, times(*first, *one), third, times(*third, *one)]
+            first = turn_cos_sin(turns[1] * r_start, SINE, COSINE)
+            right = [first, times(*first, *power(0, 2 * b + 1))]
+            left, right = (
+                jnp.concatenate([pair[c] for c in range(2) for pair in pairs], axis=0).astype(jnp.bfloat16)
+                for pairs in (left, right)
+            )
             sums_ref[b] += lax.dot_general(left, right, (((1,), (1,)), ((), ())), preferred_element_type=jnp.float32)
         return 0
 
     lax.fori_loop(0, (count + STEP - 1) // STEP, some_blocks, 0)
     for b in range(base_count):
-        sums = sums_ref[b]
-        real = sums[:SUB, :SUB] - sums[SUB:, SUB:]
-        imag = sums[:SUB, SUB:] + sums[SUB:, :SUB]
-        image_ref[0:SUB, 0:SUB] = real * samples**-0.5
-        image_ref[SUB : 2 * SUB, 0:SUB] = imag * samples**-0.5
+        image_ref[0 : 2 * SUB, 0:SUB] = sums_ref[b] * samples**-0.5
         stations = iota((ROWS - 2 * SUB, LANES), 0)
         stations = jnp.where(stations == 0, pair_ref[0, b], jnp.where(stations == 1, pair_ref[1, b], 0))
         image_ref[2 * SUB :, :] = stations.astype(jnp.float32)
@@ -155,6 +151,7 @@
             send_ref[...] = total_ref[place].astype(jnp.bfloat16)
     else:
         send_refs[0][...] = total_ref[...].astype(jnp.bfloat16)
+    copies[-1].wait()
 
 
 def split_rows(value, rows_ref, first):
@@ -173,17 +170,23 @@
     return swapped
 
 
-def subgrid_kernel(offset_hbm, table_hbm, *rest):
-    payload_refs, (pixels_ref, station_ref, table_ref, offset_ref, rows_ref, sems) = rest[:-6], rest[-6:]
-    copy = pltpu.make_async_copy(offset_hbm, offset_ref, sems.at[0])
+def subgrid_kernel(offset_hbm, *rest):
+    payload_refs, (pixels_ref, station_ref, offset_ref, rows_ref, sem) = rest[:-5], rest[-5:]
+    copy = pltpu.make_async_copy(offset_hbm, offset_ref, sem)
     copy.start()
-    table_copy = pltpu.make_async_copy(table_hbm, table_ref, sems.at[1])
-    table_copy.start()
     lane = iota((QROWS, LANES), 1)
     q = iota((QROWS, LANES), 0) * SLOTS + lane // SUB - SUB // 2
     r = lane % SUB - SUB // 2
     line = lambda h: 1.0 - (2.0 * h.astype(jnp.float32) / (SUB + 2)) ** 2
     taper = line(q) * line(r)
+    size = (LANES, LANES)
+    column, pixel = iota(size, 0) % SUB, iota(size, 1) % SUB
+    same = iota(size, 0) // SUB == iota(size, 1) // SUB
+    above = same & (pixel - SUB // 2 == column % (SUB // 2))
+    below = same & (SUB // 2 - 1 - pixel == column % (SUB // 2))
+    even = jnp.where((above | below) & (column < SUB // 2), 1.0, 0.0)
+    odd = jnp.where(column < SUB // 2, 0.0, jnp.where(below, 1.0, jnp.where(above, -1.0, 0.0)))
+    unfold = jnp.concatenate([even, odd], axis=1).astype(jnp.bfloat16)
     for g in range(pixels_ref.shape[0] // SLOTS):
         parts = []
         for ref in payload_refs:
@@ -192,9 +195,12 @@
         for part in parts[1:]:
             whole = whole + part.astype(jnp.float32)
         rows_ref[...] = whole
+        full = jnp.dot(whole[: 2 * SUB].astype(jnp.bfloat16), unfold, preferred_element_type=jnp.float32)
+        real = full[:SUB, :LANES] + full[SUB:, LANES:]
+        imag = full[SUB:, :LANES] - full[:SUB, LANES:]
         station_ref[g] = rows_ref[2 * SUB : 2 * SUB + 8, :].astype(jnp.int32)
-        real = swap([rows_ref[i * QROWS : (i + 1) * QROWS, :] for i in range(SLOTS)], lane)
-        imag = swap([rows_ref[SUB + i * QROWS : SUB + (i + 1) * QROWS, :] for i in range(SLOTS)], lane)
+        real = swap([real[i * QROWS : (i + 1) * QROWS] for i in range(SLOTS)], lane)
+        imag = swap([imag[i * QROWS : (i + 1) * QROWS] for i in range(SLOTS)], lane)
         if g == 0:
             copy.wait()
         for s in range(SLOTS):
@@ -202,7 +208,6 @@
             turn = lax.rem(offset_ref[0, slot] * q + offset_ref[1, slot] * r, SUB)
             cosine, sine = turn_cos_sin(turn.astype(jnp.float32) * (1.0 / SUB))
             pixels_ref[slot, 0], pixels_ref[slot, 1] = times(real[s], imag[s], cosine * taper, -sine * taper)
-    table_copy.wait()
 
 
 def finish_kernel(table_ref, station_ref, pixels_ref, *rest):
@@ -279,10 +284,11 @@
         sends = [jax.ShapeDtypeStruct((groups, ROWS, LANES), jnp.bfloat16)] * owners
     else:
         sends = [jax.ShapeDtypeStruct((owners, groups, ROWS, LANES), jnp.bfloat16)]
-    sent = pl.pallas_call(
+    sends.append(jax.ShapeDtypeStruct((LANES + 2 * SUB, 2 * LANES), jnp.float32))
+    *sent, table = pl.pallas_call(
         functools.partial(image_kernel, owners),
         out_shape=sends,
-        in_specs=[hbm] * 6,
+        in_specs=[hbm] * 7,
         out_specs=[vmem] * len(sends),
         scratch_shapes=[
             pltpu.SMEM((base_count,), jnp.int32),
@@ -293,19 +299,19 @@
             pltpu.VMEM(freq_ratio.shape, jnp.float32),
             pltpu.VMEM((2 * base_count, tracks.shape[-1]), jnp.float32),
             pltpu.VMEM((blocks, 2 * base_count, samples), jnp.float32),
-            pltpu.VMEM((blocks, 2 * (SLOTS - 1), 2 * base_count, samples), jnp.float32),
+            pltpu.VMEM((blocks, 4, 2 * base_count, samples), jnp.float32),
             pltpu.VMEM((owners, groups, ROWS, LANES), jnp.float32),
-            pltpu.SemaphoreType.DMA((6,)),
+            pltpu.SemaphoreType.DMA((7,)),
             pltpu.VMEM((8, LANES), jnp.float32),
             pltpu.VMEM((ROWS, LANES), jnp.float32),
-            pltpu.VMEM((base_count, 2 * SUB, 2 * SUB), jnp.float32),
+            pltpu.VMEM((base_count, 2 * SUB, SUB), jnp.float32),
             pltpu.SMEM((base_count * blocks + STEP - 1,), jnp.int32),
         ],
         compiler_params=pltpu.CompilerParams(vmem_limit_bytes=48 * 1024 * 1024),
         name="images",
-    )(*map(keep, (blocks_used, subgrid_row, station_pair.T, visibilities, tracks, freq_ratio)))
+    )(*map(keep, (blocks_used, subgrid_row, station_pair.T, visibilities, tracks, freq_ratio, tables())))
     if direct:
-        payloads = [sent[0]] + [shift_by(sent[shift], shift) for shift in range(1, owners)]
+        payloads = [sent[0]] + [shift_by(sent[shift], shift) for shift in (3,1,2)]
         payloads[0], screens[2] = lax.optimization_barrier((payloads[0], screens[2]))
         screens.append(flip(screens[2], 1))
         payloads[0], screens[1] = lax.optimization_barrier((payloads[0], screens[1]))
@@ -313,24 +319,23 @@
         by_owner = jnp.roll(sent[0], lax.axis_index("sub"), axis=0)
         payloads = [lax.all_to_all(by_owner, "sub", 0, 0, tiled=True)]
         screens = [lax.all_gather(aterm_screens, "sub", axis=1, tiled=True)]
-    subgrids, stations, table = pl.pallas_call(
+    subgrids, stations = pl.pallas_call(
         subgrid_kernel,
         out_shape=[
             jax.ShapeDtypeStruct((base_count, 2, QROWS, LANES), jnp.float32),
             jax.ShapeDtypeStruct((groups, 8, LANES), jnp.int32),
-            jax.ShapeDtypeStruct((LANES + 2 * SUB, 2 * LANES), jnp.float32),
         ],
-        in_specs=[hbm] * 2 + [vmem] * len(payloads),
-        out_specs=[vmem] * 3,
+        in_specs=[hbm] + [vmem] * len(payloads),
+        out_specs=[vmem] * 2,
         scratch_shapes=[
             pltpu.SMEM((2, base_count), jnp.int32),
             pltpu.VMEM((ROWS, LANES), jnp.float32),
-            pltpu.SemaphoreType.DMA((2,)),
+            pltpu.SemaphoreType.DMA(()),
         ],
         compiler_params=pltpu.CompilerParams(vmem_limit_bytes=48 * 1024 * 1024),
         cost_estimate=pl.CostEstimate(flops=30000000000, bytes_accessed=100000, transcendentals=0),
         name="subgrids",
-    )(keep(subgrid_offsets.T), keep(tables()), *payloads)
+    )(keep(subgrid_offsets.T), *payloads)
     return pl.pallas_call(
         finish_kernel,
         out_shape=jax.ShapeDtypeStruct((1, base_count, 2, pixels), jnp.float32),

time: 20.3 us -> 18.7 us (0.921)
  waiting for transfers between devices: 3.35 us -> 2.5 us
  Pallas kernels: 6.64 us -> 5.81 us
    ppermute x3, waiting for transfers between devices: 1.49 us -> 0.01 us  [local(): lax.ppermute(x, 'sub', [(n, n ^ bits) for n in range(owners)])]
    ppermute x3, starting transfers between devices: 3.88 us -> 2.43 us  [local(): lax.ppermute(x, 'sub', [(n, (n + shift) % owners) for n in range(owners)])]
    ppermute x3, starting transfers between devices: 6.24 us -> 7.68 us  [local(): lax.ppermute(x, 'sub', [(n, n ^ bits) for n in range(owners)])]
    pallas_call x1, Pallas kernels: 4.31 us -> 3.57 us  [local(): pl.pallas_call(functools.partial(image_kernel, owners), out_shape=sends,...]
    ppermute x3, waiting for transfers between devices: 1.86 us -> 2.49 us  [local(): lax.ppermute(x, 'sub', [(n, (n + shift) % owners) for n in range(owners)])]
  transfers between devices with their start and end apart: 6 -> 6, of which waited for: 3 -> 2; matrix products, arithmetic and copies ran while one was open for 0% -> 0% of each run, Pallas kernels for 26% -> 24%
where the time goes in v4:
time: 18.7 us; the launch traced here: 18.5 us
  starting transfers between devices  10.1 us (54%)
  Pallas kernels  5.81 us (31%)
  waiting for transfers between devices  2.5 us (13%)
    ppermute x3, starting transfers between devices, local(): lax.ppermute(x, 'sub', [(n, n ^ bits) for n in range(owners)])  7.68 us
    pallas_call x1, Pallas kernels, local(): pl.pallas_call(functools.partial(image_kernel, owners), out_shape=sends,...  3.57 us
    ppermute x3, waiting for transfers between devices, local(): lax.ppermute(x, 'sub', [(n, (n + shift) % owners) for n in range(owners)])  2.49 us
    ppermute x3, starting transfers between devices, local(): lax.ppermute(x, 'sub', [(n, (n + shift) % owners) for n in range(owners)])  2.43 us
    pallas_call x1, Pallas kernels, local(): pl.pallas_call(finish_kernel, out_shape=jax.ShapeDtypeStruct((1, base_cou...  1.35 us
    pallas_call x1, Pallas kernels, local(): pl.pallas_call(subgrid_kernel, out_shape=[jax.ShapeDtypeStruct((base_coun...  0.89 us
  transfers between devices with their start and end apart: 6, of which 2 were waited for; matrix products, arithmetic and copies ran while one was open for 0% of the time, Pallas kernels for 24%

profile of v4, /device:TPU:0, one launch (start us, length us, event | category | flops | bytes accessed | tf_op | source)
XLA Modules:
  0.0 18.5 jit_solution(17031262048218072315)
XLA Ops:
  0.0 4.0 %collective-permute-start = (bf16[1,32,2,1024]{3,2,1,0:T(2,128)(2,1)}, bf16[1,32,2,1024]{3,2,1,0:T(2,128)(2,1)S(1)}, u32[]{:S(2)}, u32[]{:S(2)}) collective-permute-start(bf16[1,32,2,1024]{3,2,1,0:T(2,128)(2,1)} %rest_0_.1), channel_id=1, source_target_pairs={{0,8},{4,12},{8,0},{12,4},{1,9},{5,13},{9,1},{13,5},{2,10},{6,14},... | collective-permute-start | bytes 393224 | tf_op jit(solution)/shard_map/ppermute | solution.py:282
  4.0 1.6 %collective-permute-start.1 = (bf16[1,32,2,1024]{3,2,1,0:T(2,128)(2,1)}, bf16[1,32,2,1024]{3,2,1,0:T(2,128)(2,1)S(1)}, u32[]{:S(2)}, u32[]{:S(2)}) collective-permute-start(bf16[1,32,2,1024]{3,2,1,0:T(2,128)(2,1)} %rest_0_.1), channel_id=1, source_target_pairs={{0,4},{4,0},{8,12},{12,8},{1,5},{5,1},{9,13},{13,9},{2,6},{6,2},{1... | collective-permute-start | bytes 393224 | tf_op jit(solution)/shard_map/ppermute | solution.py:282
  5.6 3.6 %images.1 = (bf16[1,80,128]{2,1,0:T(8,128)(2,1)S(1)}, bf16[1,80,128]{2,1,0:T(8,128)(2,1)S(1)}, bf16[1,80,128]{2,1,0:T(8,128)(2,1)S(1)}, bf16[1,80,128]{2,1,0:T(8,128)(2,1)S(1)}, f32[192,256]{1,0:T(8,128)S(1)}) custom-call(s32[4]{0:T(128)} %used_hbm.1, s32[4]{0:T(128)} %row_hbm.1, s32[2,4]{1,0:T(2,128)} %bitcast.2, bf16[1,4,8,2,1024]{4,3,2,1,0:T(2,128)(2,1)} %vis_hbm.1, ...), custom_call_target="tpu_custom_call" | custom-call | tf_op jit(solution)/shard_map/images/pallas_call | solution.py:288
  9.2 0.1 collective-permute-start.2
  9.3 2.0 %collective-permute-start.3 = (bf16[1,80,128]{2,1,0:T(8,128)(2,1)S(1)}, bf16[1,80,128]{2,1,0:T(8,128)(2,1)S(1)}, u32[]{:S(2)}, u32[]{:S(2)}) collective-permute-start(bf16[1,80,128]{2,1,0:T(8,128)(2,1)S(1)} %get-tuple-element.21), channel_id=1, source_target_pairs={{0,4},{4,8},{8,12},{12,0},{1,5},{5,9},{9,13},{13,1},{2,6},{6,10},{... | collective-permute-start | bytes 61448 | tf_op jit(solution)/shard_map/ppermute | solution.py:279
  11.3 0.4 %collective-permute-start.4 = (bf16[1,80,128]{2,1,0:T(8,128)(2,1)S(1)}, bf16[1,80,128]{2,1,0:T(8,128)(2,1)S(1)}, u32[]{:S(2)}, u32[]{:S(2)}) collective-permute-start(bf16[1,80,128]{2,1,0:T(8,128)(2,1)S(1)} %get-tuple-element.22), channel_id=1, source_target_pairs={{0,8},{4,12},{8,0},{12,4},{1,9},{5,13},{9,1},{13,5},{2,10},{6,14},... | collective-permute-start | bytes 61448 | tf_op jit(solution)/shard_map/ppermute | solution.py:279
  11.6 0.0 collective-permute-done.rest_2_
  11.6 0.0 collective-permute-done.1.rest_1_
  11.6 2.1 %collective-permute-start.5 = (bf16[1,32,2,1024]{3,2,1,0:T(2,128)(2,1)S(1)}, bf16[1,32,2,1024]{3,2,1,0:T(2,128)(2,1)S(1)}, u32[]{:S(2)}, u32[]{:S(2)}) collective-permute-start(bf16[1,32,2,1024]{3,2,1,0:T(2,128)(2,1)S(1)} %collective-permute-done.rest_2_), channel_id=1, source_target_pairs={{0,4},{4,0},{8,12},{12,8},{1,5},{5,1},{9,13},{13,9},{2,6},{6,2},{1... | collective-permute-start | bytes 393224 | tf_op jit(solution)/shard_map/ppermute | solution.py:282
  13.7 0.0 collective-permute-done.2.rest_1_
  13.7 1.3 %collective-permute-done.3.rest_2_ = bf16[1,80,128]{2,1,0:T(8,128)(2,1)S(1)} collective-permute-done((bf16[1,80,128]{2,1,0:T(8,128)(2,1)S(1)}, bf16[1,80,128]{2,1,0:T(8,128)(2,1)S(1)}, u32[]{:S(2)}, u32[]{:S(2)}) %collective-permute-start.3) | collective-permute-done | bytes 20512 | tf_op jit(solution)/shard_map/ppermute | solution.py:279
  15.0 1.2 %collective-permute-done.4.rest_3_ = bf16[1,80,128]{2,1,0:T(8,128)(2,1)S(1)} collective-permute-done((bf16[1,80,128]{2,1,0:T(8,128)(2,1)S(1)}, bf16[1,80,128]{2,1,0:T(8,128)(2,1)S(1)}, u32[]{:S(2)}, u32[]{:S(2)}) %collective-permute-start.4) | collective-permute-done | bytes 20512 | tf_op jit(solution)/shard_map/ppermute | solution.py:279
  16.2 0.0 copy-start
  16.2 0.9 %subgrids.1 = (f32[4,2,8,128]{3,2,1,0:T(8,128)S(1)}, s32[1,8,128]{2,1,0:T(8,128)S(1)}) custom-call(s32[2,4]{1,0:T(2,128)} %bitcast.3, bf16[1,80,128]{2,1,0:T(8,128)(2,1)S(1)} %get-tuple-element.19.rest_0_, bf16[1,80,128]{2,1,0:T(8,128)(2,1)S(1)} %collective-permute-done.2.rest_1_, bf16[1,80,128]{2,1,0:T(8,128)(2,1)S(1)} %collective-permute-done.3.rest_2_, ...), custom_call_target="tpu_custom_call" | custom-call | flops 30000001024 | bytes 100000 | tf_op jit(solution)/shard_map/subgrids/pallas_call | solution.py:322
  17.1 0.0 collective-permute-done.5.rest_3_
  17.1 0.0 copy-done
  17.1 1.4 %finish.1 = f32[1,4,2,1024]{3,2,1,0:T(2,128)} custom-call(f32[192,256]{1,0:T(8,128)S(1)} %get-tuple-element.16.table_ref, s32[1,8,128]{2,1,0:T(8,128)S(1)} %get-tuple-element.23.station_ref, f32[4,2,8,128]{3,2,1,0:T(8,128)S(1)} %get-tuple-element.24.pixels_ref, bf16[1,32,2,1024]{3,2,1,0:T(2,128)(2,1)S(1)} %copy-done, ...), custom_call_target="tpu_custom_call" | custom-call | tf_op jit(solution)/shard_map/finish/pallas_call | solution.py:339
Async XLA Ops:
  0.0 11.6 %collective-permute-start = (bf16[1,32,2,1024]{3,2,1,0:T(2,128)(2,1)}, bf16[1,32,2,1024]{3,2,1,0:T(2,128)(2,1)S(1)}, u32[]{:S(2)}, u32[]{:S(2)}) collective-permute-start(bf16[1,32,2,1024]{3,2,1,0:T(2,128)(2,1)} %rest_0_.1), channel_id=1, source_target_pairs={{0,8},{4,12},{8,0},{12,4},{1,9},{5,13},{9,1},{13,5},{2,10},{6,14},... | collective-permute-start | bytes 393224 | tf_op jit(solution)/shard_map/ppermute | solution.py:282
  4.0 7.6 %collective-permute-start.1 = (bf16[1,32,2,1024]{3,2,1,0:T(2,128)(2,1)}, bf16[1,32,2,1024]{3,2,1,0:T(2,128)(2,1)S(1)}, u32[]{:S(2)}, u32[]{:S(2)}) collective-permute-start(bf16[1,32,2,1024]{3,2,1,0:T(2,128)(2,1)} %rest_0_.1), channel_id=1, source_target_pairs={{0,4},{4,0},{8,12},{12,8},{1,5},{5,1},{9,13},{13,9},{2,6},{6,2},{1... | collective-permute-start | bytes 393224 | tf_op jit(solution)/shard_map/ppermute | solution.py:282
  9.2 4.5 %collective-permute-start.2 = (bf16[1,80,128]{2,1,0:T(8,128)(2,1)S(1)}, bf16[1,80,128]{2,1,0:T(8,128)(2,1)S(1)}, u32[]{:S(2)}, u32[]{:S(2)}) collective-permute-start(bf16[1,80,128]{2,1,0:T(8,128)(2,1)S(1)} %get-tuple-element.20), channel_id=1, source_target_pairs={{0,12},{4,0},{8,4},{12,8},{1,13},{5,1},{9,5},{13,9},{2,14},{6,2},{... | collective-permute-start | bytes 61448 | tf_op jit(solution)/shard_map/ppermute | solution.py:279
  9.3 5.7 %collective-permute-start.3 = (bf16[1,80,128]{2,1,0:T(8,128)(2,1)S(1)}, bf16[1,80,128]{2,1,0:T(8,128)(2,1)S(1)}, u32[]{:S(2)}, u32[]{:S(2)}) collective-permute-start(bf16[1,80,128]{2,1,0:T(8,128)(2,1)S(1)} %get-tuple-element.21), channel_id=1, source_target_pairs={{0,4},{4,8},{8,12},{12,0},{1,5},{5,9},{9,13},{13,1},{2,6},{6,10},{... | collective-permute-start | bytes 61448 | tf_op jit(solution)/shard_map/ppermute | solution.py:279
  11.3 4.9 %collective-permute-start.4 = (bf16[1,80,128]{2,1,0:T(8,128)(2,1)S(1)}, bf16[1,80,128]{2,1,0:T(8,128)(2,1)S(1)}, u32[]{:S(2)}, u32[]{:S(2)}) collective-permute-start(bf16[1,80,128]{2,1,0:T(8,128)(2,1)S(1)} %get-tuple-element.22), channel_id=1, source_target_pairs={{0,8},{4,12},{8,0},{12,4},{1,9},{5,13},{9,1},{13,5},{2,10},{6,14},... | collective-permute-start | bytes 61448 | tf_op jit(solution)/shard_map/ppermute | solution.py:279
  11.6 5.5 %collective-permute-start.5 = (bf16[1,32,2,1024]{3,2,1,0:T(2,128)(2,1)S(1)}, bf16[1,32,2,1024]{3,2,1,0:T(2,128)(2,1)S(1)}, u32[]{:S(2)}, u32[]{:S(2)}) collective-permute-start(bf16[1,32,2,1024]{3,2,1,0:T(2,128)(2,1)S(1)} %collective-permute-done.rest_2_), channel_id=1, source_target_pairs={{0,4},{4,0},{8,12},{12,8},{1,5},{5,1},{9,13},{13,9},{2,6},{6,2},{1... | collective-permute-start | bytes 393224 | tf_op jit(solution)/shard_map/ppermute | solution.py:282
  16.2 0.9 %copy-start = (bf16[1,32,2,1024]{3,2,1,0:T(2,128)(2,1)S(1)}, bf16[1,32,2,1024]{3,2,1,0:T(2,128)(2,1)}, u32[]{:S(2)}) copy-start(bf16[1,32,2,1024]{3,2,1,0:T(2,128)(2,1)} %rest_0_.1) | copy-start | bytes 393220

commit v5 on v4

--- a/solution.py
+++ b/solution.py
@@ -3,6 +3,7 @@
 
 import jax
 import jax.numpy as jnp
+import numpy as np
 from jax import lax
 from jax.experimental import pallas as pl
 from jax.experimental.pallas import tpu as pltpu
@@ -13,8 +14,7 @@
 SLOTS = LANES // SUB
 QROWS = SUB // SLOTS
 ROWS = 2 * SUB + 16
-STEP = 8
-HIGHEST = lax.Precision.HIGHEST
+STEP = 16
 SINE = (3.14159027, -5.16740673, 2.54401052, -0.55946246)
 COSINE = (0.99999325, -4.93393467, 4.0412481, -1.22203176)
 SINE_LONG = (3.14159264, -5.16771008, 2.55007752, -0.59829129, 0.07765766)
@@ -44,12 +44,17 @@
     return lax.broadcasted_iota(jnp.int32, shape, axis)
 
 
+def pixel_lines():
+    lane = iota((QROWS, LANES), 1)
+    return iota((QROWS, LANES), 0) * SLOTS + lane // SUB - SUB // 2, lane % SUB - SUB // 2
+
+
 def image_kernel(
-    axis_size, used_hbm, row_hbm, pair_hbm, vis_hbm, tracks_hbm, freq_hbm, table_hbm, *rest
+    axis_size, used_hbm, row_hbm, pair_hbm, vis_hbm, tracks_hbm, freq_hbm, offset_hbm, table_hbm, *rest
 ):
-    send_refs, table_ref, scratch = rest[:-16], rest[-16], rest[-15:]
+    send_refs, (centre_ref, table_ref), scratch = rest[:-18], rest[-18:-16], rest[-16:]
     (used_ref, row_ref, pair_ref, vis_ref, tracks_ref, freq_ref, lines_ref, turns_ref, powers_ref, total_ref,
-     sems, wide_ref, image_ref, sums_ref, block_ref) = scratch
+     sems, wide_ref, image_ref, sums_ref, block_ref, offset_ref) = scratch
     base_count, blocks, _, samples = vis_ref.shape
     channels = freq_ref.shape[1]
     steps = samples // channels
@@ -59,7 +64,8 @@
     tiles = samples // LANES
     sources = (
         (tracks_hbm, tracks_ref), (freq_hbm, freq_ref), (used_hbm, used_ref), (vis_hbm.at[0], vis_ref),
-        (row_hbm, row_ref), (pair_hbm, pair_ref), (table_hbm, table_ref),
+        (row_hbm, row_ref), (pair_hbm, pair_ref), (offset_hbm, offset_ref),
+        (table_hbm, table_ref),
     )
     copies = [pltpu.make_async_copy(one, two, sems.at[n]) for n, (one, two) in enumerate(sources)]
     for copy in copies:
@@ -96,6 +102,15 @@
     r_start = iota((QROWS, 1), 0).astype(jnp.float32) + 0.5
     for copy in copies[2:-1]:
         copy.wait()
+
+    q, r = pixel_lines()
+    line = lambda h: 1.0 - (2.0 * h.astype(jnp.float32) / (SUB + 2)) ** 2
+    taper = line(q) * line(r)
+    for slot in range(base_count):
+        turn = lax.rem(offset_ref[0, slot] * q + offset_ref[1, slot] * r, SUB)
+        cosine, sine = turn_cos_sin(turn.astype(jnp.float32) * (1.0 / SUB))
+        centre_ref[slot, 0] = cosine * taper
+        centre_ref[slot, 1] = -sine * taper
 
     count = jnp.int32(0)
     for b in range(base_count):
@@ -159,6 +174,11 @@
         rows_ref[first + 2 * a : first + 2 * a + 2, :] = value[:, a * LANES : (a + 1) * LANES]
 
 
+def halves(value):
+    high = value.astype(jnp.bfloat16)
+    return high, (value - high.astype(jnp.float32)).astype(jnp.bfloat16)
+
+
 def swap(parts, lane):
     swapped = []
     for s in range(SLOTS):
@@ -170,15 +190,9 @@
     return swapped
 
 
-def subgrid_kernel(offset_hbm, *rest):
-    payload_refs, (pixels_ref, station_ref, offset_ref, rows_ref, sem) = rest[:-5], rest[-5:]
-    copy = pltpu.make_async_copy(offset_hbm, offset_ref, sem)
-    copy.start()
+def subgrid_kernel(centre_ref, *rest):
+    payload_refs, (pixels_ref, station_ref) = rest[:-2], rest[-2:]
     lane = iota((QROWS, LANES), 1)
-    q = iota((QROWS, LANES), 0) * SLOTS + lane // SUB - SUB // 2
-    r = lane % SUB - SUB // 2
-    line = lambda h: 1.0 - (2.0 * h.astype(jnp.float32) / (SUB + 2)) ** 2
-    taper = line(q) * line(r)
     size = (LANES, LANES)
     column, pixel = iota(size, 0) % SUB, iota(size, 1) % SUB
     same = iota(size, 0) // SUB == iota(size, 1) // SUB
@@ -194,24 +208,20 @@
         whole = parts[0].astype(jnp.float32)
         for part in parts[1:]:
             whole = whole + part.astype(jnp.float32)
-        rows_ref[...] = whole
         full = jnp.dot(whole[: 2 * SUB].astype(jnp.bfloat16), unfold, preferred_element_type=jnp.float32)
         real = full[:SUB, :LANES] + full[SUB:, LANES:]
         imag = full[SUB:, :LANES] - full[:SUB, LANES:]
-        station_ref[g] = rows_ref[2 * SUB : 2 * SUB + 8, :].astype(jnp.int32)
+        station_ref[g] = whole[2 * SUB : 2 * SUB + 8].astype(jnp.int32)
         real = swap([real[i * QROWS : (i + 1) * QROWS] for i in range(SLOTS)], lane)
         imag = swap([imag[i * QROWS : (i + 1) * QROWS] for i in range(SLOTS)], lane)
-        if g == 0:
-            copy.wait()
         for s in range(SLOTS):
             slot = g * SLOTS + s
-            turn = lax.rem(offset_ref[0, slot] * q + offset_ref[1, slot] * r, SUB)
-            cosine, sine = turn_cos_sin(turn.astype(jnp.float32) * (1.0 / SUB))
-            pixels_ref[slot, 0], pixels_ref[slot, 1] = times(real[s], imag[s], cosine * taper, -sine * taper)
+            pixels_ref[slot, 0], pixels_ref[slot, 1] = times(real[s], imag[s], centre_ref[slot, 0], centre_ref[slot, 1])
 
 
 def finish_kernel(table_ref, station_ref, pixels_ref, *rest):
     screens_refs, (out_ref, screen_ref) = rest[:-2], rest[-2:]
+    second = table_ref.shape[0] // 2
     me = lax.axis_index("sub")
     lane = iota((QROWS, LANES), 1)
 
@@ -240,11 +250,18 @@
             weighted.append(times(pixels_ref[slot, 0], pixels_ref[slot, 1], *gain))
         planes = swap([pair[0] for pair in weighted], lane) + swap([pair[1] for pair in weighted], lane)
         planes = jnp.concatenate(planes, axis=0)
-        half = jnp.dot(planes, table_ref[:LANES], precision=HIGHEST, preferred_element_type=jnp.float32)
+        high, low = halves(planes)
+        wide = jnp.dot(jnp.concatenate([high, low], axis=0), table_ref[:LANES], preferred_element_type=jnp.float32)
+        half = wide[: 2 * SUB] + wide[2 * SUB :]
+        half = half + jnp.dot(high, table_ref[second : second + LANES], preferred_element_type=jnp.float32)
         half_real = half[:SUB, :LANES] + half[SUB:, LANES:]
         half_imag = half[SUB:, :LANES] - half[:SUB, LANES:]
         half = jnp.concatenate([half_real, half_imag], axis=0)
-        full = jnp.dot(table_ref[LANES:, : 2 * SUB], half, precision=HIGHEST, preferred_element_type=jnp.float32)
+        high, low = halves(half)
+        q_high = table_ref[LANES:second, : 2 * SUB]
+        q_low = table_ref[second + LANES :, : 2 * SUB]
+        wide = jnp.dot(q_high, jnp.concatenate([high, low], axis=1), preferred_element_type=jnp.float32)
+        full = wide[:, :LANES] + wide[:, LANES:] + jnp.dot(q_low, high, preferred_element_type=jnp.float32)
         for c in range(2):
             flat = swap([full[c * SUB + i * QROWS : c * SUB + (i + 1) * QROWS] for i in range(SLOTS)], lane)
             for s in range(SLOTS):
@@ -263,7 +280,9 @@
     cos = [[turn(math.cos, x, y) / SUB for y in order] for x in order]
     sin = [[turn(math.sin, x, y) / SUB for y in order] for x in order]
     q_table = [c + s for c, s in zip(cos, sin)] + [[-v for v in s] + c for c, s in zip(cos, sin)]
-    return jnp.array(r_table + [row + [0.0] * (2 * LANES - 2 * SUB) for row in q_table], jnp.float32)
+    table = np.array(r_table + [row + [0.0] * (2 * LANES - 2 * SUB) for row in q_table], np.float32)
+    high = table.astype(jnp.bfloat16)
+    return jnp.array(np.concatenate([high, (table - high.astype(np.float32)).astype(jnp.bfloat16)], axis=0))
 
 
 def local(
@@ -284,11 +303,12 @@
         sends = [jax.ShapeDtypeStruct((groups, ROWS, LANES), jnp.bfloat16)] * owners
     else:
         sends = [jax.ShapeDtypeStruct((owners, groups, ROWS, LANES), jnp.bfloat16)]
-    sends.append(jax.ShapeDtypeStruct((LANES + 2 * SUB, 2 * LANES), jnp.float32))
-    *sent, table = pl.pallas_call(
+    sends.append(jax.ShapeDtypeStruct((base_count, 2, QROWS, LANES), jnp.float32))
+    sends.append(jax.ShapeDtypeStruct((2 * (LANES + 2 * SUB), 2 * LANES), jnp.bfloat16))
+    *sent, centre, table = pl.pallas_call(
         functools.partial(image_kernel, owners),
         out_shape=sends,
-        in_specs=[hbm] * 7,
+        in_specs=[hbm] * 8,
         out_specs=[vmem] * len(sends),
         scratch_shapes=[
             pltpu.SMEM((base_count,), jnp.int32),
@@ -301,17 +321,18 @@
             pltpu.VMEM((blocks, 2 * base_count, samples), jnp.float32),
             pltpu.VMEM((blocks, 4, 2 * base_count, samples), jnp.float32),
             pltpu.VMEM((owners, groups, ROWS, LANES), jnp.float32),
-            pltpu.SemaphoreType.DMA((7,)),
+            pltpu.SemaphoreType.DMA((8,)),
             pltpu.VMEM((8, LANES), jnp.float32),
             pltpu.VMEM((ROWS, LANES), jnp.float32),
             pltpu.VMEM((base_count, 2 * SUB, SUB), jnp.float32),
             pltpu.SMEM((base_count * blocks + STEP - 1,), jnp.int32),
+            pltpu.SMEM((2, base_count), jnp.int32),
         ],
         compiler_params=pltpu.CompilerParams(vmem_limit_bytes=48 * 1024 * 1024),
         name="images",
-    )(*map(keep, (blocks_used, subgrid_row, station_pair.T, visibilities, tracks, freq_ratio, tables())))
+    )(*map(keep, (blocks_used, subgrid_row, station_pair.T, visibilities, tracks, freq_ratio, subgrid_offsets.T, tables())))
     if direct:
-        payloads = [sent[0]] + [shift_by(sent[shift], shift) for shift in (3,1,2)]
+        payloads = [sent[0]] + [shift_by(sent[shift], shift) for shift in (3, 1, 2)]
         payloads[0], screens[2] = lax.optimization_barrier((payloads[0], screens[2]))
         screens.append(flip(screens[2], 1))
         payloads[0], screens[1] = lax.optimization_barrier((payloads[0], screens[1]))
@@ -325,17 +346,12 @@
             jax.ShapeDtypeStruct((base_count, 2, QROWS, LANES), jnp.float32),
             jax.ShapeDtypeStruct((groups, 8, LANES), jnp.int32),
         ],
-        in_specs=[hbm] + [vmem] * len(payloads),
+        in_specs=[vmem] * (1 + len(payloads)),
         out_specs=[vmem] * 2,
-        scratch_shapes=[
-            pltpu.SMEM((2, base_count), jnp.int32),
-            pltpu.VMEM((ROWS, LANES), jnp.float32),
-            pltpu.SemaphoreType.DMA(()),
-        ],
         compiler_params=pltpu.CompilerParams(vmem_limit_bytes=48 * 1024 * 1024),
-        cost_estimate=pl.CostEstimate(flops=30000000000, bytes_accessed=100000, transcendentals=0),
+        cost_estimate=pl.CostEstimate(flops=10000000000, bytes_accessed=100000, transcendentals=0),
         name="subgrids",
-    )(keep(subgrid_offsets.T), *payloads)
+    )(centre, *payloads)
     return pl.pallas_call(
         finish_kernel,
         out_shape=jax.ShapeDtypeStruct((1, base_count, 2, pixels), jnp.float32),

time: 18.7 us -> 18.5 us (0.989)
  Pallas kernels: 5.81 us -> 5.07 us
  waiting for transfers between devices: 2.5 us -> 2.92 us
  local copies, waits for them, and re-layouts: 0.01 us -> 0.22 us
    pallas_call x1, Pallas kernels: 0.89 us -> 0.23 us  [local(): pl.pallas_call(subgrid_kernel, out_shape=[jax.ShapeDtypeStruct((base_coun...]
    ppermute x3, waiting for transfers between devices: 0.01 us -> 0.45 us  [local(): lax.ppermute(x, 'sub', [(n, n ^ bits) for n in range(owners)])]
    unnamed x2, local copies, waits for them, and re-layouts: 0.01 us -> 0.22 us
  transfers between devices with their start and end apart: 6 -> 6, of which waited for: 2 -> 3; matrix products, arithmetic and copies ran while one was open for 0% -> 0% of each run, Pallas kernels for 24% -> 21%
where the time goes in v5:
time: 18.5 us; the launch traced here: 18.4 us
  starting transfers between devices  10.1 us (55%)
  Pallas kernels  5.07 us (27%)
  waiting for transfers between devices  2.92 us (16%)
  local copies, waits for them, and re-layouts  0.22 us (1%)
    ppermute x3, starting transfers between devices, local(): lax.ppermute(x, 'sub', [(n, n ^ bits) for n in range(owners)])  7.7 us
    pallas_call x1, Pallas kernels, local(): pl.pallas_call(functools.partial(image_kernel, owners), out_shape=sends,...  3.55 us
    ppermute x3, waiting for transfers between devices, local(): lax.ppermute(x, 'sub', [(n, (n + shift) % owners) for n in range(owners)])  2.48 us
    ppermute x3, starting transfers between devices, local(): lax.ppermute(x, 'sub', [(n, (n + shift) % owners) for n in range(owners)])  2.41 us
    pallas_call x1, Pallas kernels, local(): pl.pallas_call(finish_kernel, out_shape=jax.ShapeDtypeStruct((1, base_cou...  1.28 us
    ppermute x3, waiting for transfers between devices, local(): lax.ppermute(x, 'sub', [(n, n ^ bits) for n in range(owners)])  0.45 us
  transfers between devices with their start and end apart: 6, of which 3 were waited for; matrix products, arithmetic and copies ran while one was open for 0% of the time, Pallas kernels for 21%

profile of v5, /device:TPU:0, one launch (start us, length us, event | category | flops | bytes accessed | tf_op | source)
XLA Modules:
  0.0 18.4 jit_solution(12109328507468150885)
XLA Ops:
  0.0 4.0 %collective-permute-start = (bf16[1,32,2,1024]{3,2,1,0:T(2,128)(2,1)}, bf16[1,32,2,1024]{3,2,1,0:T(2,128)(2,1)S(1)}, u32[]{:S(2)}, u32[]{:S(2)}) collective-permute-start(bf16[1,32,2,1024]{3,2,1,0:T(2,128)(2,1)} %rest_0_.1), channel_id=1, source_target_pairs={{0,8},{4,12},{8,0},{12,4},{1,9},{5,13},{9,1},{13,5},{2,10},{6,14},... | collective-permute-start | bytes 393224 | tf_op jit(solution)/shard_map/ppermute | solution.py:301
  4.0 1.6 %collective-permute-start.1 = (bf16[1,32,2,1024]{3,2,1,0:T(2,128)(2,1)}, bf16[1,32,2,1024]{3,2,1,0:T(2,128)(2,1)S(1)}, u32[]{:S(2)}, u32[]{:S(2)}) collective-permute-start(bf16[1,32,2,1024]{3,2,1,0:T(2,128)(2,1)} %rest_0_.1), channel_id=1, source_target_pairs={{0,4},{4,0},{8,12},{12,8},{1,5},{5,1},{9,13},{13,9},{2,6},{6,2},{1... | collective-permute-start | bytes 393224 | tf_op jit(solution)/shard_map/ppermute | solution.py:301
  5.6 3.6 %images.1 = (bf16[1,80,128]{2,1,0:T(8,128)(2,1)S(1)}, bf16[1,80,128]{2,1,0:T(8,128)(2,1)S(1)}, bf16[1,80,128]{2,1,0:T(8,128)(2,1)S(1)}, bf16[1,80,128]{2,1,0:T(8...) custom-call(s32[4]{0:T(128)} %used_hbm.1, s32[4]{0:T(128)} %row_hbm.1, s32[2,4]{1,0:T(2,128)} %bitcast.2, ...), custom_call_target="tpu_custom_call" | custom-call | tf_op jit(solution)/shard_map/images/pallas_call | solution.py:308
  9.2 0.1 collective-permute-start.2
  9.2 2.0 %collective-permute-start.3 = (bf16[1,80,128]{2,1,0:T(8,128)(2,1)S(1)}, bf16[1,80,128]{2,1,0:T(8,128)(2,1)S(1)}, u32[]{:S(2)}, u32[]{:S(2)}) collective-permute-start(bf16[1,80,128]{2,1,0:T(8,128)(2,1)S(1)} %get-tuple-element.23), channel_id=1, source_target_pairs={{0,4},{4,8},{8,12},{12,0},{1,5},{5,9},{9,13},{13,1},{2,6},{6,10},{... | collective-permute-start | bytes 61448 | tf_op jit(solution)/shard_map/ppermute | solution.py:298
  11.3 0.3 %collective-permute-start.4 = (bf16[1,80,128]{2,1,0:T(8,128)(2,1)S(1)}, bf16[1,80,128]{2,1,0:T(8,128)(2,1)S(1)}, u32[]{:S(2)}, u32[]{:S(2)}) collective-permute-start(bf16[1,80,128]{2,1,0:T(8,128)(2,1)S(1)} %get-tuple-element.24), channel_id=1, source_target_pairs={{0,8},{4,12},{8,0},{12,4},{1,9},{5,13},{9,1},{13,5},{2,10},{6,14},... | collective-permute-start | bytes 61448 | tf_op jit(solution)/shard_map/ppermute | solution.py:298
  11.6 0.0 collective-permute-done.rest_2_
  11.6 0.0 collective-permute-done.1.rest_1_
  11.6 2.1 %collective-permute-start.5 = (bf16[1,32,2,1024]{3,2,1,0:T(2,128)(2,1)S(1)}, bf16[1,32,2,1024]{3,2,1,0:T(2,128)(2,1)S(1)}, u32[]{:S(2)}, u32[]{:S(2)}) collective-permute-start(bf16[1,32,2,1024]{3,2,1,0:T(2,128)(2,1)S(1)} %collective-permute-done.rest_2_), channel_id=1, source_target_pairs={{0,4},{4,0},{8,12},{12,8},{1,5},{5,1},{9,13},{13,9},{2,6},{6,2},{1... | collective-permute-start | bytes 393224 | tf_op jit(solution)/shard_map/ppermute | solution.py:301
  13.7 0.0 collective-permute-done.2.rest_1_
  13.7 1.3 %collective-permute-done.3.rest_2_ = bf16[1,80,128]{2,1,0:T(8,128)(2,1)S(1)} collective-permute-done((bf16[1,80,128]{2,1,0:T(8,128)(2,1)S(1)}, bf16[1,80,128]{2,1,0:T(8,128)(2,1)S(1)}, u32[]{:S(2)}, u32[]{:S(2)}) %collective-permute-start.3) | collective-permute-done | bytes 20512 | tf_op jit(solution)/shard_map/ppermute | solution.py:298
  15.0 1.2 %collective-permute-done.4.rest_3_ = bf16[1,80,128]{2,1,0:T(8,128)(2,1)S(1)} collective-permute-done((bf16[1,80,128]{2,1,0:T(8,128)(2,1)S(1)}, bf16[1,80,128]{2,1,0:T(8,128)(2,1)S(1)}, u32[]{:S(2)}, u32[]{:S(2)}) %collective-permute-start.4) | collective-permute-done | bytes 20512 | tf_op jit(solution)/shard_map/ppermute | solution.py:298
  16.2 0.0 copy-start
  16.2 0.2 %subgrids.1 = (f32[4,2,8,128]{3,2,1,0:T(8,128)S(1)}, s32[1,8,128]{2,1,0:T(8,128)S(1)}) custom-call(f32[4,2,8,128]{3,2,1,0:T(8,128)S(1)} %get-tuple-element.18.centre_ref, bf16[1,80,128]{2,1,0:T(8,128)(2,1)S(1)} %get-tuple-element.21.rest_0_, bf16[1,80,128]{2,1,0:T(8,128)(2,1)S(1)} %collective-permute-done.2.rest_1_, ...), custom_call_target="tpu_custom_call" | custom-call | flops 10000000000 | bytes 100000 | tf_op jit(solution)/shard_map/subgrids/pallas_call | solution.py:343
  16.4 0.4 %collective-permute-done.5.rest_3_ = bf16[1,32,2,1024]{3,2,1,0:T(2,128)(2,1)S(1)} collective-permute-done((bf16[1,32,2,1024]{3,2,1,0:T(2,128)(2,1)S(1)}, bf16[1,32,2,1024]{3,2,1,0:T(2,128)(2,1)S(1)}, u32[]{:S(2)}, u32[]{:S(2)}) %collective-permute-start.5) | collective-permute-done | bytes 131104 | tf_op jit(solution)/shard_map/ppermute | solution.py:301
  16.9 0.2 %copy-done = bf16[1,32,2,1024]{3,2,1,0:T(2,128)(2,1)S(1)} copy-done((bf16[1,32,2,1024]{3,2,1,0:T(2,128)(2,1)S(1)}, bf16[1,32,2,1024]{3,2,1,0:T(2,128)(2,1)}, u32[]{:S(2)}) %copy-start) | copy-done | bytes 131096
  17.1 1.3 %finish.1 = f32[1,4,2,1024]{3,2,1,0:T(2,128)} custom-call(bf16[384,256]{1,0:T(8,128)(2,1)S(1)} %get-tuple-element.17.table_ref, s32[1,8,128]{2,1,0:T(8,128)S(1)} %get-tuple-element.25.station_ref, f32[4,2,8,128]{3,2,1,0:T(8,128)S(1)} %get-tuple-element.26.pixels_ref, bf16[1,32,2,1024]{3,2,1,0:T(2,128)(2,1)S(1)} %copy-done, ...), custom_call_target="tpu_custom_call" | custom-call | tf_op jit(solution)/shard_map/finish/pallas_call | solution.py:355
Async XLA Ops:
  0.0 11.6 %collective-permute-start = (bf16[1,32,2,1024]{3,2,1,0:T(2,128)(2,1)}, bf16[1,32,2,1024]{3,2,1,0:T(2,128)(2,1)S(1)}, u32[]{:S(2)}, u32[]{:S(2)}) collective-permute-start(bf16[1,32,2,1024]{3,2,1,0:T(2,128)(2,1)} %rest_0_.1), channel_id=1, source_target_pairs={{0,8},{4,12},{8,0},{12,4},{1,9},{5,13},{9,1},{13,5},{2,10},{6,14},... | collective-permute-start | bytes 393224 | tf_op jit(solution)/shard_map/ppermute | solution.py:301
  4.0 7.6 %collective-permute-start.1 = (bf16[1,32,2,1024]{3,2,1,0:T(2,128)(2,1)}, bf16[1,32,2,1024]{3,2,1,0:T(2,128)(2,1)S(1)}, u32[]{:S(2)}, u32[]{:S(2)}) collective-permute-start(bf16[1,32,2,1024]{3,2,1,0:T(2,128)(2,1)} %rest_0_.1), channel_id=1, source_target_pairs={{0,4},{4,0},{8,12},{12,8},{1,5},{5,1},{9,13},{13,9},{2,6},{6,2},{1... | collective-permute-start | bytes 393224 | tf_op jit(solution)/shard_map/ppermute | solution.py:301
  9.2 4.5 %collective-permute-start.2 = (bf16[1,80,128]{2,1,0:T(8,128)(2,1)S(1)}, bf16[1,80,128]{2,1,0:T(8,128)(2,1)S(1)}, u32[]{:S(2)}, u32[]{:S(2)}) collective-permute-start(bf16[1,80,128]{2,1,0:T(8,128)(2,1)S(1)} %get-tuple-element.22), channel_id=1, source_target_pairs={{0,12},{4,0},{8,4},{12,8},{1,13},{5,1},{9,5},{13,9},{2,14},{6,2},{... | collective-permute-start | bytes 61448 | tf_op jit(solution)/shard_map/ppermute | solution.py:298
  9.2 5.7 %collective-permute-start.3 = (bf16[1,80,128]{2,1,0:T(8,128)(2,1)S(1)}, bf16[1,80,128]{2,1,0:T(8,128)(2,1)S(1)}, u32[]{:S(2)}, u32[]{:S(2)}) collective-permute-start(bf16[1,80,128]{2,1,0:T(8,128)(2,1)S(1)} %get-tuple-element.23), channel_id=1, source_target_pairs={{0,4},{4,8},{8,12},{12,0},{1,5},{5,9},{9,13},{13,1},{2,6},{6,10},{... | collective-permute-start | bytes 61448 | tf_op jit(solution)/shard_map/ppermute | solution.py:298
  11.3 4.9 %collective-permute-start.4 = (bf16[1,80,128]{2,1,0:T(8,128)(2,1)S(1)}, bf16[1,80,128]{2,1,0:T(8,128)(2,1)S(1)}, u32[]{:S(2)}, u32[]{:S(2)}) collective-permute-start(bf16[1,80,128]{2,1,0:T(8,128)(2,1)S(1)} %get-tuple-element.24), channel_id=1, source_target_pairs={{0,8},{4,12},{8,0},{12,4},{1,9},{5,13},{9,1},{13,5},{2,10},{6,14},... | collective-permute-start | bytes 61448 | tf_op jit(solution)/shard_map/ppermute | solution.py:298
  11.6 5.3 %collective-permute-start.5 = (bf16[1,32,2,1024]{3,2,1,0:T(2,128)(2,1)S(1)}, bf16[1,32,2,1024]{3,2,1,0:T(2,128)(2,1)S(1)}, u32[]{:S(2)}, u32[]{:S(2)}) collective-permute-start(bf16[1,32,2,1024]{3,2,1,0:T(2,128)(2,1)S(1)} %collective-permute-done.rest_2_), channel_id=1, source_target_pairs={{0,4},{4,0},{8,12},{12,8},{1,5},{5,1},{9,13},{13,9},{2,6},{6,2},{1... | collective-permute-start | bytes 393224 | tf_op jit(solution)/shard_map/ppermute | solution.py:301
  16.2 0.9 %copy-start = (bf16[1,32,2,1024]{3,2,1,0:T(2,128)(2,1)S(1)}, bf16[1,32,2,1024]{3,2,1,0:T(2,128)(2,1)}, u32[]{:S(2)}) copy-start(bf16[1,32,2,1024]{3,2,1,0:T(2,128)(2,1)} %rest_0_.1) | copy-start | bytes 393220

commit v6 on v5

--- a/solution.py
+++ b/solution.py
@@ -230,9 +230,9 @@
             return screens_refs[0][0, station]
         here = screens_refs[0].shape[1]
         away = me ^ (station // here)
-        value = screens_refs[0][0, station % here]
+        value = screens_refs[0][0, station % here].astype(jnp.float32)
         for flips in range(1, len(screens_refs)):
-            value = jnp.where(away == flips, screens_refs[flips][0, station % here], value)
+            value = jnp.where(away == flips, screens_refs[flips][0, station % here].astype(jnp.float32), value)
         return value
 
     for g in range(pixels_ref.shape[0] // SLOTS):

time: 18.5 us -> 18.5 us (level)
  no operation moved by 1% of the time
where the time goes in v6:
time: 18.5 us; the launch traced here: 18.3 us
  starting transfers between devices  10.1 us (55%)
  Pallas kernels  5.06 us (27%)
  waiting for transfers between devices  2.92 us (16%)
  local copies, waits for them, and re-layouts  0.21 us (1%)
    ppermute x3, starting transfers between devices, local(): lax.ppermute(x, 'sub', [(n, n ^ bits) for n in range(owners)])  7.74 us
    pallas_call x1, Pallas kernels, local(): pl.pallas_call(functools.partial(image_kernel, owners), out_shape=sends,...  3.56 us
    ppermute x3, waiting for transfers between devices, local(): lax.ppermute(x, 'sub', [(n, (n + shift) % owners) for n in range(owners)])  2.47 us
    ppermute x3, starting transfers between devices, local(): lax.ppermute(x, 'sub', [(n, (n + shift) % owners) for n in range(owners)])  2.37 us
    pallas_call x1, Pallas kernels, local(): pl.pallas_call(finish_kernel, out_shape=jax.ShapeDtypeStruct((1, base_cou...  1.27 us
    ppermute x3, waiting for transfers between devices, local(): lax.ppermute(x, 'sub', [(n, n ^ bits) for n in range(owners)])  0.45 us
  transfers between devices with their start and end apart: 6, of which 3 were waited for; matrix products, arithmetic and copies ran while one was open for 0% of the time, Pallas kernels for 21%

profile of v6, /device:TPU:0, one launch (start us, length us, event | category | flops | bytes accessed | tf_op | source)
XLA Modules:
  0.0 18.3 jit_solution(14439594597898562207)
XLA Ops:
  0.0 4.0 %collective-permute-start = (bf16[1,32,2,1024]{3,2,1,0:T(2,128)(2,1)}, bf16[1,32,2,1024]{3,2,1,0:T(2,128)(2,1)S(1)}, u32[]{:S(2)}, u32[]{:S(2)}) collective-permute-start(bf16[1,32,2,1024]{3,2,1,0:T(2,128)(2,1)} %rest_0_.1), channel_id=1, source_target_pairs={{0,8},{4,12},{8,0},{12,4},{1,9},{5,13},{9,1},{13,5},{2,10},{6,14},... | collective-permute-start | bytes 393224 | tf_op jit(solution)/shard_map/ppermute | solution.py:301
  4.0 1.6 %collective-permute-start.1 = (bf16[1,32,2,1024]{3,2,1,0:T(2,128)(2,1)}, bf16[1,32,2,1024]{3,2,1,0:T(2,128)(2,1)S(1)}, u32[]{:S(2)}, u32[]{:S(2)}) collective-permute-start(bf16[1,32,2,1024]{3,2,1,0:T(2,128)(2,1)} %rest_0_.1), channel_id=1, source_target_pairs={{0,4},{4,0},{8,12},{12,8},{1,5},{5,1},{9,13},{13,9},{2,6},{6,2},{1... | collective-permute-start | bytes 393224 | tf_op jit(solution)/shard_map/ppermute | solution.py:301
  5.6 3.6 %images.1 = (bf16[1,80,128]{2,1,0:T(8,128)(2,1)S(1)}, bf16[1,80,128]{2,1,0:T(8,128)(2,1)S(1)}, bf16[1,80,128]{2,1,0:T(8,128)(2,1)S(1)}, bf16[1,80,128]{2,1,0:T(8...) custom-call(s32[4]{0:T(128)} %used_hbm.1, s32[4]{0:T(128)} %row_hbm.1, s32[2,4]{1,0:T(2,128)} %bitcast.2, ...), custom_call_target="tpu_custom_call" | custom-call | tf_op jit(solution)/shard_map/images/pallas_call | solution.py:308
  9.2 0.1 collective-permute-start.2
  9.2 2.0 %collective-permute-start.3 = (bf16[1,80,128]{2,1,0:T(8,128)(2,1)S(1)}, bf16[1,80,128]{2,1,0:T(8,128)(2,1)S(1)}, u32[]{:S(2)}, u32[]{:S(2)}) collective-permute-start(bf16[1,80,128]{2,1,0:T(8,128)(2,1)S(1)} %get-tuple-element.23), channel_id=1, source_target_pairs={{0,4},{4,8},{8,12},{12,0},{1,5},{5,9},{9,13},{13,1},{2,6},{6,10},{... | collective-permute-start | bytes 61448 | tf_op jit(solution)/shard_map/ppermute | solution.py:298
  11.3 0.3 %collective-permute-start.4 = (bf16[1,80,128]{2,1,0:T(8,128)(2,1)S(1)}, bf16[1,80,128]{2,1,0:T(8,128)(2,1)S(1)}, u32[]{:S(2)}, u32[]{:S(2)}) collective-permute-start(bf16[1,80,128]{2,1,0:T(8,128)(2,1)S(1)} %get-tuple-element.24), channel_id=1, source_target_pairs={{0,8},{4,12},{8,0},{12,4},{1,9},{5,13},{9,1},{13,5},{2,10},{6,14},... | collective-permute-start | bytes 61448 | tf_op jit(solution)/shard_map/ppermute | solution.py:298
  11.6 0.0 collective-permute-done.rest_2_
  11.6 0.0 collective-permute-done.1.rest_1_
  11.6 2.1 %collective-permute-start.5 = (bf16[1,32,2,1024]{3,2,1,0:T(2,128)(2,1)S(1)}, bf16[1,32,2,1024]{3,2,1,0:T(2,128)(2,1)S(1)}, u32[]{:S(2)}, u32[]{:S(2)}) collective-permute-start(bf16[1,32,2,1024]{3,2,1,0:T(2,128)(2,1)S(1)} %collective-permute-done.rest_2_), channel_id=1, source_target_pairs={{0,4},{4,0},{8,12},{12,8},{1,5},{5,1},{9,13},{13,9},{2,6},{6,2},{1... | collective-permute-start | bytes 393224 | tf_op jit(solution)/shard_map/ppermute | solution.py:301
  13.7 0.0 collective-permute-done.2.rest_1_
  13.7 1.3 %collective-permute-done.3.rest_2_ = bf16[1,80,128]{2,1,0:T(8,128)(2,1)S(1)} collective-permute-done((bf16[1,80,128]{2,1,0:T(8,128)(2,1)S(1)}, bf16[1,80,128]{2,1,0:T(8,128)(2,1)S(1)}, u32[]{:S(2)}, u32[]{:S(2)}) %collective-permute-start.3) | collective-permute-done | bytes 20512 | tf_op jit(solution)/shard_map/ppermute | solution.py:298
  15.0 1.2 %collective-permute-done.4.rest_3_ = bf16[1,80,128]{2,1,0:T(8,128)(2,1)S(1)} collective-permute-done((bf16[1,80,128]{2,1,0:T(8,128)(2,1)S(1)}, bf16[1,80,128]{2,1,0:T(8,128)(2,1)S(1)}, u32[]{:S(2)}, u32[]{:S(2)}) %collective-permute-start.4) | collective-permute-done | bytes 20512 | tf_op jit(solution)/shard_map/ppermute | solution.py:298
  16.2 0.0 copy-start
  16.2 0.2 %subgrids.1 = (f32[4,2,8,128]{3,2,1,0:T(8,128)S(1)}, s32[1,8,128]{2,1,0:T(8,128)S(1)}) custom-call(f32[4,2,8,128]{3,2,1,0:T(8,128)S(1)} %get-tuple-element.18.centre_ref, bf16[1,80,128]{2,1,0:T(8,128)(2,1)S(1)} %get-tuple-element.21.rest_0_, bf16[1,80,128]{2,1,0:T(8,128)(2,1)S(1)} %collective-permute-done.2.rest_1_, ...), custom_call_target="tpu_custom_call" | custom-call | flops 10000000000 | bytes 100000 | tf_op jit(solution)/shard_map/subgrids/pallas_call | solution.py:343
  16.4 0.4 %collective-permute-done.5.rest_3_ = bf16[1,32,2,1024]{3,2,1,0:T(2,128)(2,1)S(1)} collective-permute-done((bf16[1,32,2,1024]{3,2,1,0:T(2,128)(2,1)S(1)}, bf16[1,32,2,1024]{3,2,1,0:T(2,128)(2,1)S(1)}, u32[]{:S(2)}, u32[]{:S(2)}) %collective-permute-start.5) | collective-permute-done | bytes 131104 | tf_op jit(solution)/shard_map/ppermute | solution.py:301
  16.9 0.2 %copy-done = bf16[1,32,2,1024]{3,2,1,0:T(2,128)(2,1)S(1)} copy-done((bf16[1,32,2,1024]{3,2,1,0:T(2,128)(2,1)S(1)}, bf16[1,32,2,1024]{3,2,1,0:T(2,128)(2,1)}, u32[]{:S(2)}) %copy-start) | copy-done | bytes 131096
  17.1 1.3 %finish.1 = f32[1,4,2,1024]{3,2,1,0:T(2,128)} custom-call(bf16[384,256]{1,0:T(8,128)(2,1)S(1)} %get-tuple-element.17.table_ref, s32[1,8,128]{2,1,0:T(8,128)S(1)} %get-tuple-element.25.station_ref, f32[4,2,8,128]{3,2,1,0:T(8,128)S(1)} %get-tuple-element.26.pixels_ref, bf16[1,32,2,1024]{3,2,1,0:T(2,128)(2,1)S(1)} %copy-done, ...), custom_call_target="tpu_custom_call" | custom-call | tf_op jit(solution)/shard_map/finish/pallas_call | solution.py:355
Async XLA Ops:
  0.0 11.6 %collective-permute-start = (bf16[1,32,2,1024]{3,2,1,0:T(2,128)(2,1)}, bf16[1,32,2,1024]{3,2,1,0:T(2,128)(2,1)S(1)}, u32[]{:S(2)}, u32[]{:S(2)}) collective-permute-start(bf16[1,32,2,1024]{3,2,1,0:T(2,128)(2,1)} %rest_0_.1), channel_id=1, source_target_pairs={{0,8},{4,12},{8,0},{12,4},{1,9},{5,13},{9,1},{13,5},{2,10},{6,14},... | collective-permute-start | bytes 393224 | tf_op jit(solution)/shard_map/ppermute | solution.py:301
  4.0 7.5 %collective-permute-start.1 = (bf16[1,32,2,1024]{3,2,1,0:T(2,128)(2,1)}, bf16[1,32,2,1024]{3,2,1,0:T(2,128)(2,1)S(1)}, u32[]{:S(2)}, u32[]{:S(2)}) collective-permute-start(bf16[1,32,2,1024]{3,2,1,0:T(2,128)(2,1)} %rest_0_.1), channel_id=1, source_target_pairs={{0,4},{4,0},{8,12},{12,8},{1,5},{5,1},{9,13},{13,9},{2,6},{6,2},{1... | collective-permute-start | bytes 393224 | tf_op jit(solution)/shard_map/ppermute | solution.py:301
  9.2 4.5 %collective-permute-start.2 = (bf16[1,80,128]{2,1,0:T(8,128)(2,1)S(1)}, bf16[1,80,128]{2,1,0:T(8,128)(2,1)S(1)}, u32[]{:S(2)}, u32[]{:S(2)}) collective-permute-start(bf16[1,80,128]{2,1,0:T(8,128)(2,1)S(1)} %get-tuple-element.22), channel_id=1, source_target_pairs={{0,12},{4,0},{8,4},{12,8},{1,13},{5,1},{9,5},{13,9},{2,14},{6,2},{... | collective-permute-start | bytes 61448 | tf_op jit(solution)/shard_map/ppermute | solution.py:298
  9.2 5.7 %collective-permute-start.3 = (bf16[1,80,128]{2,1,0:T(8,128)(2,1)S(1)}, bf16[1,80,128]{2,1,0:T(8,128)(2,1)S(1)}, u32[]{:S(2)}, u32[]{:S(2)}) collective-permute-start(bf16[1,80,128]{2,1,0:T(8,128)(2,1)S(1)} %get-tuple-element.23), channel_id=1, source_target_pairs={{0,4},{4,8},{8,12},{12,0},{1,5},{5,9},{9,13},{13,1},{2,6},{6,10},{... | collective-permute-start | bytes 61448 | tf_op jit(solution)/shard_map/ppermute | solution.py:298
  11.3 4.9 %collective-permute-start.4 = (bf16[1,80,128]{2,1,0:T(8,128)(2,1)S(1)}, bf16[1,80,128]{2,1,0:T(8,128)(2,1)S(1)}, u32[]{:S(2)}, u32[]{:S(2)}) collective-permute-start(bf16[1,80,128]{2,1,0:T(8,128)(2,1)S(1)} %get-tuple-element.24), channel_id=1, source_target_pairs={{0,8},{4,12},{8,0},{12,4},{1,9},{5,13},{9,1},{13,5},{2,10},{6,14},... | collective-permute-start | bytes 61448 | tf_op jit(solution)/shard_map/ppermute | solution.py:298
  11.6 5.3 %collective-permute-start.5 = (bf16[1,32,2,1024]{3,2,1,0:T(2,128)(2,1)S(1)}, bf16[1,32,2,1024]{3,2,1,0:T(2,128)(2,1)S(1)}, u32[]{:S(2)}, u32[]{:S(2)}) collective-permute-start(bf16[1,32,2,1024]{3,2,1,0:T(2,128)(2,1)S(1)} %collective-permute-done.rest_2_), channel_id=1, source_target_pairs={{0,4},{4,0},{8,12},{12,8},{1,5},{5,1},{9,13},{13,9},{2,6},{6,2},{1... | collective-permute-start | bytes 393224 | tf_op jit(solution)/shard_map/ppermute | solution.py:301
  16.2 0.9 %copy-start = (bf16[1,32,2,1024]{3,2,1,0:T(2,128)(2,1)S(1)}, bf16[1,32,2,1024]{3,2,1,0:T(2,128)(2,1)}, u32[]{:S(2)}) copy-start(bf16[1,32,2,1024]{3,2,1,0:T(2,128)(2,1)} %rest_0_.1) | copy-start | bytes 393220

commit v7 on v6

--- a/solution.py
+++ b/solution.py
@@ -70,11 +70,14 @@
     copies = [pltpu.make_async_copy(one, two, sems.at[n]) for n, (one, two) in enumerate(sources)]
     for copy in copies:
         copy.start()
+    total_ref[...] = jnp.zeros_like(total_ref)
+    sums_ref[...] = jnp.zeros_like(sums_ref)
+    wide_ref[...] = jnp.zeros_like(wide_ref)
+
     copies[0].wait()
     copies[1].wait()
     for b in range(base_count):
         lines_ref[2 * b : 2 * b + 2, :] = tracks_ref[b]
-    wide_ref[...] = jnp.zeros_like(wide_ref)
     wide_ref[0:1, :channels] = freq_ref[...]
     wide = jnp.broadcast_to(wide_ref[0:1, :], (8, LANES))
     lane = iota((8, LANES), 1)
@@ -96,8 +99,6 @@
         return 0
 
     lax.fori_loop(0, blocks, prepare, 0, unroll=blocks if lines <= 8 else 1)
-    total_ref[...] = jnp.zeros_like(total_ref)
-    sums_ref[...] = jnp.zeros_like(sums_ref)
     q_start = (iota((QROWS, 1), 0) * SLOTS - SUB // 2).astype(jnp.float32)
     r_start = iota((QROWS, 1), 0).astype(jnp.float32) + 0.5
     for copy in copies[2:-1]:

time: 18.5 us -> 18.5 us (level)
  no operation moved by 1% of the time
where the time goes in v7:
time: 18.5 us; the launch traced here: 18.3 us
  starting transfers between devices  10.1 us (55%)
  Pallas kernels  5.05 us (27%)
  waiting for transfers between devices  2.92 us (16%)
  local copies, waits for them, and re-layouts  0.19 us (1%)
    ppermute x3, starting transfers between devices, local(): lax.ppermute(x, 'sub', [(n, n ^ bits) for n in range(owners)])  7.71 us
    pallas_call x1, Pallas kernels, local(): pl.pallas_call(functools.partial(image_kernel, owners), out_shape=sends,...  3.54 us
    ppermute x3, waiting for transfers between devices, local(): lax.ppermute(x, 'sub', [(n, (n + shift) % owners) for n in range(owners)])  2.45 us
    ppermute x3, starting transfers between devices, local(): lax.ppermute(x, 'sub', [(n, (n + shift) % owners) for n in range(owners)])  2.41 us
    pallas_call x1, Pallas kernels, local(): pl.pallas_call(finish_kernel, out_shape=jax.ShapeDtypeStruct((1, base_cou...  1.28 us
    ppermute x3, waiting for transfers between devices, local(): lax.ppermute(x, 'sub', [(n, n ^ bits) for n in range(owners)])  0.47 us
  transfers between devices with their start and end apart: 6, of which 3 were waited for; matrix products, arithmetic and copies ran while one was open for 0% of the time, Pallas kernels for 21%

profile of v7, /device:TPU:0, one launch (start us, length us, event | category | flops | bytes accessed | tf_op | source)
XLA Modules:
  0.0 18.3 jit_solution(18301551340546634822)
XLA Ops:
  0.0 4.0 %collective-permute-start = (bf16[1,32,2,1024]{3,2,1,0:T(2,128)(2,1)}, bf16[1,32,2,1024]{3,2,1,0:T(2,128)(2,1)S(1)}, u32[]{:S(2)}, u32[]{:S(2)}) collective-permute-start(bf16[1,32,2,1024]{3,2,1,0:T(2,128)(2,1)} %rest_0_.1), channel_id=1, source_target_pairs={{0,8},{4,12},{8,0},{12,4},{1,9},{5,13},{9,1},{13,5},{2,10},{6,14},... | collective-permute-start | bytes 393224 | tf_op jit(solution)/shard_map/ppermute | solution.py:302
  4.0 1.6 %collective-permute-start.1 = (bf16[1,32,2,1024]{3,2,1,0:T(2,128)(2,1)}, bf16[1,32,2,1024]{3,2,1,0:T(2,128)(2,1)S(1)}, u32[]{:S(2)}, u32[]{:S(2)}) collective-permute-start(bf16[1,32,2,1024]{3,2,1,0:T(2,128)(2,1)} %rest_0_.1), channel_id=1, source_target_pairs={{0,4},{4,0},{8,12},{12,8},{1,5},{5,1},{9,13},{13,9},{2,6},{6,2},{1... | collective-permute-start | bytes 393224 | tf_op jit(solution)/shard_map/ppermute | solution.py:302
  5.6 3.5 %images.1 = (bf16[1,80,128]{2,1,0:T(8,128)(2,1)S(1)}, bf16[1,80,128]{2,1,0:T(8,128)(2,1)S(1)}, bf16[1,80,128]{2,1,0:T(8,128)(2,1)S(1)}, bf16[1,80,128]{2,1,0:T(8...) custom-call(s32[4]{0:T(128)} %used_hbm.1, s32[4]{0:T(128)} %row_hbm.1, s32[2,4]{1,0:T(2,128)} %bitcast.2, ...), custom_call_target="tpu_custom_call" | custom-call | tf_op jit(solution)/shard_map/images/pallas_call | solution.py:309
  9.2 0.1 collective-permute-start.2
  9.2 2.0 %collective-permute-start.3 = (bf16[1,80,128]{2,1,0:T(8,128)(2,1)S(1)}, bf16[1,80,128]{2,1,0:T(8,128)(2,1)S(1)}, u32[]{:S(2)}, u32[]{:S(2)}) collective-permute-start(bf16[1,80,128]{2,1,0:T(8,128)(2,1)S(1)} %get-tuple-element.23), channel_id=1, source_target_pairs={{0,4},{4,8},{8,12},{12,0},{1,5},{5,9},{9,13},{13,1},{2,6},{6,10},{... | collective-permute-start | bytes 61448 | tf_op jit(solution)/shard_map/ppermute | solution.py:299
  11.2 0.3 %collective-permute-start.4 = (bf16[1,80,128]{2,1,0:T(8,128)(2,1)S(1)}, bf16[1,80,128]{2,1,0:T(8,128)(2,1)S(1)}, u32[]{:S(2)}, u32[]{:S(2)}) collective-permute-start(bf16[1,80,128]{2,1,0:T(8,128)(2,1)S(1)} %get-tuple-element.24), channel_id=1, source_target_pairs={{0,8},{4,12},{8,0},{12,4},{1,9},{5,13},{9,1},{13,5},{2,10},{6,14},... | collective-permute-start | bytes 61448 | tf_op jit(solution)/shard_map/ppermute | solution.py:299
  11.6 0.0 collective-permute-done.rest_2_
  11.6 0.0 collective-permute-done.1.rest_1_
  11.6 2.1 %collective-permute-start.5 = (bf16[1,32,2,1024]{3,2,1,0:T(2,128)(2,1)S(1)}, bf16[1,32,2,1024]{3,2,1,0:T(2,128)(2,1)S(1)}, u32[]{:S(2)}, u32[]{:S(2)}) collective-permute-start(bf16[1,32,2,1024]{3,2,1,0:T(2,128)(2,1)S(1)} %collective-permute-done.rest_2_), channel_id=1, source_target_pairs={{0,4},{4,0},{8,12},{12,8},{1,5},{5,1},{9,13},{13,9},{2,6},{6,2},{1... | collective-permute-start | bytes 393224 | tf_op jit(solution)/shard_map/ppermute | solution.py:302
  13.7 0.0 collective-permute-done.2.rest_1_
  13.7 1.3 %collective-permute-done.3.rest_2_ = bf16[1,80,128]{2,1,0:T(8,128)(2,1)S(1)} collective-permute-done((bf16[1,80,128]{2,1,0:T(8,128)(2,1)S(1)}, bf16[1,80,128]{2,1,0:T(8,128)(2,1)S(1)}, u32[]{:S(2)}, u32[]{:S(2)}) %collective-permute-start.3) | collective-permute-done | bytes 20512 | tf_op jit(solution)/shard_map/ppermute | solution.py:299
  15.0 1.2 %collective-permute-done.4.rest_3_ = bf16[1,80,128]{2,1,0:T(8,128)(2,1)S(1)} collective-permute-done((bf16[1,80,128]{2,1,0:T(8,128)(2,1)S(1)}, bf16[1,80,128]{2,1,0:T(8,128)(2,1)S(1)}, u32[]{:S(2)}, u32[]{:S(2)}) %collective-permute-start.4) | collective-permute-done | bytes 20512 | tf_op jit(solution)/shard_map/ppermute | solution.py:299
  16.1 0.0 copy-start
  16.1 0.2 %subgrids.1 = (f32[4,2,8,128]{3,2,1,0:T(8,128)S(1)}, s32[1,8,128]{2,1,0:T(8,128)S(1)}) custom-call(f32[4,2,8,128]{3,2,1,0:T(8,128)S(1)} %get-tuple-element.18.centre_ref, bf16[1,80,128]{2,1,0:T(8,128)(2,1)S(1)} %get-tuple-element.21.rest_0_, bf16[1,80,128]{2,1,0:T(8,128)(2,1)S(1)} %collective-permute-done.2.rest_1_, ...), custom_call_target="tpu_custom_call" | custom-call | flops 10000000000 | bytes 100000 | tf_op jit(solution)/shard_map/subgrids/pallas_call | solution.py:344
  16.4 0.5 %collective-permute-done.5.rest_3_ = bf16[1,32,2,1024]{3,2,1,0:T(2,128)(2,1)S(1)} collective-permute-done((bf16[1,32,2,1024]{3,2,1,0:T(2,128)(2,1)S(1)}, bf16[1,32,2,1024]{3,2,1,0:T(2,128)(2,1)S(1)}, u32[]{:S(2)}, u32[]{:S(2)}) %collective-permute-start.5) | collective-permute-done | bytes 131104 | tf_op jit(solution)/shard_map/ppermute | solution.py:302
  16.8 0.2 %copy-done = bf16[1,32,2,1024]{3,2,1,0:T(2,128)(2,1)S(1)} copy-done((bf16[1,32,2,1024]{3,2,1,0:T(2,128)(2,1)S(1)}, bf16[1,32,2,1024]{3,2,1,0:T(2,128)(2,1)}, u32[]{:S(2)}) %copy-start) | copy-done | bytes 131096
  17.0 1.3 %finish.1 = f32[1,4,2,1024]{3,2,1,0:T(2,128)} custom-call(bf16[384,256]{1,0:T(8,128)(2,1)S(1)} %get-tuple-element.17.table_ref, s32[1,8,128]{2,1,0:T(8,128)S(1)} %get-tuple-element.25.station_ref, f32[4,2,8,128]{3,2,1,0:T(8,128)S(1)} %get-tuple-element.26.pixels_ref, bf16[1,32,2,1024]{3,2,1,0:T(2,128)(2,1)S(1)} %copy-done, ...), custom_call_target="tpu_custom_call" | custom-call | tf_op jit(solution)/shard_map/finish/pallas_call | solution.py:356
Async XLA Ops:
  0.0 11.6 %collective-permute-start = (bf16[1,32,2,1024]{3,2,1,0:T(2,128)(2,1)}, bf16[1,32,2,1024]{3,2,1,0:T(2,128)(2,1)S(1)}, u32[]{:S(2)}, u32[]{:S(2)}) collective-permute-start(bf16[1,32,2,1024]{3,2,1,0:T(2,128)(2,1)} %rest_0_.1), channel_id=1, source_target_pairs={{0,8},{4,12},{8,0},{12,4},{1,9},{5,13},{9,1},{13,5},{2,10},{6,14},... | collective-permute-start | bytes 393224 | tf_op jit(solution)/shard_map/ppermute | solution.py:302
  4.0 7.5 %collective-permute-start.1 = (bf16[1,32,2,1024]{3,2,1,0:T(2,128)(2,1)}, bf16[1,32,2,1024]{3,2,1,0:T(2,128)(2,1)S(1)}, u32[]{:S(2)}, u32[]{:S(2)}) collective-permute-start(bf16[1,32,2,1024]{3,2,1,0:T(2,128)(2,1)} %rest_0_.1), channel_id=1, source_target_pairs={{0,4},{4,0},{8,12},{12,8},{1,5},{5,1},{9,13},{13,9},{2,6},{6,2},{1... | collective-permute-start | bytes 393224 | tf_op jit(solution)/shard_map/ppermute | solution.py:302
  9.2 4.5 %collective-permute-start.2 = (bf16[1,80,128]{2,1,0:T(8,128)(2,1)S(1)}, bf16[1,80,128]{2,1,0:T(8,128)(2,1)S(1)}, u32[]{:S(2)}, u32[]{:S(2)}) collective-permute-start(bf16[1,80,128]{2,1,0:T(8,128)(2,1)S(1)} %get-tuple-element.22), channel_id=1, source_target_pairs={{0,12},{4,0},{8,4},{12,8},{1,13},{5,1},{9,5},{13,9},{2,14},{6,2},{... | collective-permute-start | bytes 61448 | tf_op jit(solution)/shard_map/ppermute | solution.py:299
  9.2 5.7 %collective-permute-start.3 = (bf16[1,80,128]{2,1,0:T(8,128)(2,1)S(1)}, bf16[1,80,128]{2,1,0:T(8,128)(2,1)S(1)}, u32[]{:S(2)}, u32[]{:S(2)}) collective-permute-start(bf16[1,80,128]{2,1,0:T(8,128)(2,1)S(1)} %get-tuple-element.23), channel_id=1, source_target_pairs={{0,4},{4,8},{8,12},{12,0},{1,5},{5,9},{9,13},{13,1},{2,6},{6,10},{... | collective-permute-start | bytes 61448 | tf_op jit(solution)/shard_map/ppermute | solution.py:299
  11.2 4.9 %collective-permute-start.4 = (bf16[1,80,128]{2,1,0:T(8,128)(2,1)S(1)}, bf16[1,80,128]{2,1,0:T(8,128)(2,1)S(1)}, u32[]{:S(2)}, u32[]{:S(2)}) collective-permute-start(bf16[1,80,128]{2,1,0:T(8,128)(2,1)S(1)} %get-tuple-element.24), channel_id=1, source_target_pairs={{0,8},{4,12},{8,0},{12,4},{1,9},{5,13},{9,1},{13,5},{2,10},{6,14},... | collective-permute-start | bytes 61448 | tf_op jit(solution)/shard_map/ppermute | solution.py:299
  11.6 5.3 %collective-permute-start.5 = (bf16[1,32,2,1024]{3,2,1,0:T(2,128)(2,1)S(1)}, bf16[1,32,2,1024]{3,2,1,0:T(2,128)(2,1)S(1)}, u32[]{:S(2)}, u32[]{:S(2)}) collective-permute-start(bf16[1,32,2,1024]{3,2,1,0:T(2,128)(2,1)S(1)} %collective-permute-done.rest_2_), channel_id=1, source_target_pairs={{0,4},{4,0},{8,12},{12,8},{1,5},{5,1},{9,13},{13,9},{2,6},{6,2},{1... | collective-permute-start | bytes 393224 | tf_op jit(solution)/shard_map/ppermute | solution.py:302
  16.1 0.9 %copy-start = (bf16[1,32,2,1024]{3,2,1,0:T(2,128)(2,1)S(1)}, bf16[1,32,2,1024]{3,2,1,0:T(2,128)(2,1)}, u32[]{:S(2)}) copy-start(bf16[1,32,2,1024]{3,2,1,0:T(2,128)(2,1)} %rest_0_.1) | copy-start | bytes 393220
